TPU v7x, 512 devices: a whole 4x4x16 slice. The times are simulated.
512 devices in a mesh: grp: 16 (over y, x_lo, core), seq: 32 (over x_hi, z).
Axes of the slice: x: 4 (x_hi: 2, x_lo: 2; x = x_hi * 2 + x_lo), y: 4, z: 16, core: 2. Of those that a mesh axis runs over, the one named last changes fastest.
Arguments:
- query_heads: bfloat16 [128, 12, 512, 128], P('grp', None, 'seq'), may hold values from -40 to 40
- key_heads: bfloat16 [128, 12, 512, 128], P('grp', None, 'seq'), may hold values from -40 to 40
- value_heads: bfloat16 [128, 12, 512, 128], P('grp', None, 'seq'), may hold values from -8 to 8
- residual: bfloat16 [128, 512, 1536], P('grp', 'seq'), may hold values from -16 to 16
- modulation: bfloat16 [128, 4, 1536], P('grp'), may hold values from 0.099609375 to 1.8984375
- router: bfloat16 [1536, 32], replicated, may hold values from -0.15625 to 0.15625
- up_proj: bfloat16 [32, 2048, 1536], P('seq', 'grp'), may hold values from -0.15625 to 0.15625
- down_proj: bfloat16 [32, 2048, 1536], P('seq', 'grp'), may hold values from -0.125 to 0.125
- expert_ids: int32 [16, 32, 128, 2], P('grp', 'seq'), may hold values from 0 to 31, all different within a row; in each aligned block of 128 rows (0 to 127, 128 to 255, ..., all dimensions but the last counted through in order) at most 16 rows name the same one
Outputs:
- output: bfloat16 [128, 512, 1536], P('grp', 'seq')
Inputs may be any that keep to these rules, and one draw needn't show every extreme that they name: `expert_ids`: each token names two different experts. Among the 128 tokens of one device no expert is named by more than 16 of them, and in every draw some device names some expert exactly 16 times.
All inputs are finite; a program needn't handle non-finite values.
Results may differ from a plain program's by a relative error of at most 0.012.
Values may be sent and summed in bfloat16 or wider, within the bound.
No kernel may reach another device: no remote copies, remote signals or barrier semaphores. Data moves between devices by JAX's collectives and lax.ppermute only.
A program may use at most 64 MiB of HBM per device.

v0:
```python
import math

import jax
import jax.numpy as jnp
from jax import lax
from jax.sharding import PartitionSpec as P

norm_eps = 1e-06


def attend_items(pieces):
    queries, key_rows, values = pieces
    item_count = queries.shape[1]
    length = queries.shape[2]
    head_width = queries.shape[3]
    block_rows = min(length, 512)
    block_count = length // block_rows
    scale_factor_term = 1.0 / math.sqrt(head_width)
    query_blocks = (
        queries[0].reshape(item_count, block_count, block_rows, head_width).transpose(1, 0, 2, 3)
    )

    def one_block(query_block):
        attention_scores = (
            jnp.einsum("kld,kmd->klm", query_block, key_rows[0], preferred_element_type=jnp.float32)
            * scale_factor_term
        )
        weight_matrix_set = jax.nn.softmax(attention_scores, axis=-1).astype(jnp.bfloat16)
        return jnp.einsum(
            "klm,kmd->kld", weight_matrix_set, values[0], preferred_element_type=jnp.float32
        ).astype(jnp.bfloat16)

    outputs = lax.map(one_block, query_blocks)
    merged = outputs.transpose(1, 0, 2, 3).reshape(1, item_count, length, head_width)
    return lax.all_to_all(merged, "seq", split_axis=2, concat_axis=0, tiled=True)


def per_device(
    query_heads,
    key_heads,
    value_heads,
    residual,
    modulation,
    router,
    up_proj,
    down_proj,
    expert_ids,
):
    seqs_dev, head_count, len_dev, head_width = query_heads.shape
    group_indices = lax.axis_size("seq")
    pair_count = seqs_dev * head_count // group_indices
    tok_dev = seqs_dev * len_dev
    model_width = head_count * head_width

    def arrange(array):
        return array.reshape(group_indices, pair_count, len_dev, head_width)

    attended = attend_items(
        (
            lax.all_to_all(arrange(query_heads), "seq", split_axis=0, concat_axis=2, tiled=True),
            lax.all_to_all(arrange(key_heads), "seq", split_axis=0, concat_axis=2, tiled=True),
            lax.all_to_all(arrange(value_heads), "seq", split_axis=0, concat_axis=2, tiled=True),
        )
    )
    attn_tok = (
        attended.reshape(seqs_dev, head_count, len_dev, head_width)
        .transpose(0, 2, 1, 3)
        .reshape(seqs_dev, len_dev, model_width)
    )
    modulators = modulation.astype(jnp.float32)
    stream = (
        residual.astype(jnp.float32) + modulators[:, 0:1, :] * attn_tok.astype(jnp.float32)
    ).astype(jnp.bfloat16)
    widened = stream.astype(jnp.float32)
    center = jnp.mean(widened, axis=-1, keepdims=True)
    spread = jnp.mean(jnp.square(widened - center), axis=-1, keepdims=True)
    normed = (
        (widened - center) * lax.rsqrt(spread + norm_eps) * modulators[:, 1:2, :]
        + modulators[:, 2:3, :]
    ).astype(jnp.bfloat16)
    tokens = normed.reshape(tok_dev, model_width)
    chosen = expert_ids.reshape(tok_dev, 2)
    logits = jnp.dot(tokens, router, preferred_element_type=jnp.float32)
    picked = jnp.take_along_axis(logits, chosen, axis=1)
    lifted = jax.nn.sigmoid(picked)
    gate_mix = lifted / jnp.sum(lifted, axis=1, keepdims=True)
    experts = router.shape[1]
    capacity = 4 * tok_dev // experts
    flat_ids = chosen.reshape(-1)
    onehot = (flat_ids[:, None] == jnp.arange(experts, dtype=jnp.int32)[None, :]).astype(jnp.int32)
    running = jnp.cumsum(onehot, axis=0)
    slot_index = jnp.sum(running * onehot, axis=1) - 1
    target = (flat_ids * capacity + slot_index).reshape(tok_dev, 2)
    places = jnp.arange(experts * capacity, dtype=jnp.int32)[:, None]
    placing = ((places == target[None, :, 0]) | (places == target[None, :, 1])).astype(jnp.bfloat16)
    outbound = (
        jnp.dot(placing, tokens, preferred_element_type=jnp.float32)
        .astype(jnp.bfloat16)
        .reshape(experts, capacity, model_width)
    )
    inbound = lax.all_to_all(outbound, "seq", split_axis=0, concat_axis=0, tiled=True)
    arrived = inbound.reshape(group_indices * capacity, model_width)
    up_local = up_proj[0]
    down_local = down_proj[0]
    up_piece = lax.all_gather(up_local, "grp", axis=0, tiled=True)
    down_piece = lax.all_gather(down_local, "grp", axis=0, tiled=True)
    pre_act = lax.dot_general(
        arrived, up_piece, (((1,), (1,)), ((), ())), preferred_element_type=jnp.float32
    )
    hidden = jax.nn.gelu(pre_act).astype(jnp.bfloat16)
    summed = jnp.dot(hidden, down_piece, preferred_element_type=jnp.float32)
    results = summed.astype(jnp.bfloat16)
    returned = lax.all_to_all(
        results.reshape(group_indices, capacity, model_width),
        "seq",
        split_axis=0,
        concat_axis=0,
        tiled=True,
    )
    slots_back = returned.reshape(experts * capacity, model_width)
    fetched = slots_back[target]
    moe_sum = jnp.sum(gate_mix[:, :, None] * fetched.astype(jnp.float32), axis=1)
    output = (
        widened + modulators[:, 3:4, :] * moe_sum.reshape(seqs_dev, len_dev, model_width)
    ).astype(jnp.bfloat16)
    return output


def solution(mesh):
    return jax.shard_map(
        per_device,
        mesh=mesh,
        in_specs=(
            P("grp", None, "seq", None),
            P("grp", None, "seq", None),
            P("grp", None, "seq", None),
            P("grp", "seq", None),
            P("grp", None, None),
            P(),
            P("seq", "grp", None),
            P("seq", "grp", None),
            P("grp", "seq", None, None),
        ),
        out_specs=P("grp", "seq", None),
        check_vma=False,
    )
```

profile of v0, /device:TPU:40, one launch (start us, length us, event | category | flops | bytes accessed | tf_op | source)
XLA Modules:
  0.0 354.2 jit_solution(8799704950124048109)
XLA Ops:
  6.5 0.0 copy-start
  6.5 0.0 copy-start.3
  6.5 0.0 all-gather.5.cloned.1.call-start
  6.5 0.7 all-gather.5.cloned.1.call-update
  7.3 45.9 %all_to_all.67 = bf16[32,3,16,128]{3,2,1,0:T(8,128)(2,1)S(1)} all-to-all(bf16[32,3,16,128]{3,2,1,0:T(8,128)(2,1)} %bitcast.121), channel_id=1, replica_groups=mesh['grp'=16,'seq'=32] {'seq'}, dimensions={0} | all-to-all | bytes 786432 | tf_op jit(solution)/shard_map/all_to_all | solution.py:60
  53.1 32.4 %all_to_all.68 = bf16[32,3,16,128]{3,2,1,0:T(8,128)(2,1)S(1)} all-to-all(bf16[32,3,16,128]{3,2,1,0:T(8,128)(2,1)} %bitcast.122), channel_id=1, replica_groups=mesh['grp'=16,'seq'=32] {'seq'}, dimensions={0} | all-to-all | bytes 786432 | tf_op jit(solution)/shard_map/all_to_all | solution.py:61
  85.5 4.2 %all-to-all-start.2 = ((bf16[32,3,16,128]{3,2,1,0:T(8,128)(2,1)}), bf16[32,3,16,128]{3,2,1,0:T(8,128)(2,1)S(1)}, u32[]{:S(2)}, u32[]{:S(2)}) async-start(bf16[32,3,16,128]{3,2,1,0:T(8,128)(2,1)} %bitcast.123), calls=%async_computation.2 | async-start | bytes 786432 | tf_op jit(solution)/shard_map/all_to_all | solution.py:62
  89.7 0.0 all-gather.7.cloned.1.call-start
  89.8 0.7 all-gather.7.cloned.1.call-update
  90.5 0.0 copy-done.3
  90.5 0.1 copy.74
  90.6 0.1 eq.60
  90.7 0.1 eq.56
  90.9 0.6 reduce-window.6
  91.5 0.2 slice_reduce_fusion
  91.7 0.1 fusion.47
  91.9 25.9 %all-to-all-done.2 = bf16[32,3,16,128]{3,2,1,0:T(8,128)(2,1)S(1)} async-done(((bf16[32,3,16,128]{3,2,1,0:T(8,128)(2,1)}), bf16[32,3,16,128]{3,2,1,0:T(8,128)(2,1)S(1)}, u32[]{:S(2)}, u32[]{:S(2)}) %all-to-all-start.2) | async-done | bytes 393248 | tf_op jit(solution)/shard_map/all_to_all | solution.py:62
  117.9 2.8 fusion.57
  120.7 0.0 copy-start.2
  120.7 2.7 fusion.24
  123.4 0.0 copy-start.1
  123.4 1.2 copy.70
  124.6 4.3 %all-to-all-start.3 = ((bf16[1,3,512,128]{3,1,0,2:T(4,128)(2,1)}), bf16[1,3,512,128]{3,1,0,2:T(4,128)(2,1)S(1)}, u32[]{:S(2)}, u32[]{:S(2)}) async-start(bf16[1,3,512,128]{3,1,0,2:T(4,128)(2,1)} %copy.70), calls=%async_computation.3 | async-start | bytes 1048576 | tf_op jit(solution)/shard_map/all_to_all | solution.py:35
  128.8 0.1 sub.37
  129.0 0.1 copy.80
  129.1 0.0 copy-done.2
  129.1 33.4 %all-to-all-done.3 = bf16[1,3,512,128]{3,1,0,2:T(4,128)(2,1)S(1)} async-done(((bf16[1,3,512,128]{3,1,0,2:T(4,128)(2,1)}), bf16[1,3,512,128]{3,1,0,2:T(4,128)(2,1)S(1)}, u32[]{:S(2)}, u32[]{:S(2)}) %all-to-all-start.3) | async-done | bytes 393248 | tf_op jit(solution)/shard_map/all_to_all | solution.py:35
  162.6 0.1 copy.71
  162.7 0.1 convert_bitcast_fusion
  162.7 0.1 copy.72
  162.8 0.0 copy-done.1
  162.8 0.2 convert_reduce_fusion
  163.0 0.3 fusion.29
  163.3 0.4 fusion.32
  163.6 0.6 convolution_convert_fusion
  164.2 82.8 %all_to_all.69 = bf16[32,16,1536]{2,1,0:T(8,128)(2,1)S(1)} all-to-all(bf16[32,16,1536]{2,1,0:T(8,128)(2,1)S(1)} %bitcast.110), channel_id=1, replica_groups=mesh['grp'=16,'seq'=32] {'seq'}, dimensions={0} | all-to-all | bytes 3145728 | tf_op jit(solution)/shard_map/all_to_all | solution.py:101
  247.0 0.0 all-gather.5.cloned.1.call-done
  247.0 0.0 all-gather.7.cloned.1.call-done
  247.0 12.5 %fusion.13 = bf16[512,1536]{1,0:T(8,128)(2,1)} fusion(bf16[1,2048,1536]{2,1,0:T(8,128)(2,1)} %all-gather.7.cloned.1.call-done, bf16[512,1536]{1,0:T(8,128)(2,1)S(1)} %bitcast.116, bf16[1,2048,1536]{2,1,0:T(8,128)(2,1)} %all-gather.5.cloned.1.call-done), kind=kOutput, calls=%fused_computation.18 | convolution fusion | flops 6452674560 | bytes 15728640 | tf_op jit(solution)/shard_map/dot_general | solution.py:111
  259.5 4.1 %all-to-all-start.5 = ((bf16[32,16,1536]{2,1,0:T(8,128)(2,1)}), bf16[32,16,1536]{2,1,0:T(8,128)(2,1)S(1)}, u32[]{:S(2)}, u32[]{:S(2)}) async-start(bf16[32,16,1536]{2,1,0:T(8,128)(2,1)} %bitcast.115), calls=%async_computation.5 | async-start | bytes 3145728 | tf_op jit(solution)/shard_map/all_to_all | solution.py:113
  263.6 0.1 sub.38
  263.8 0.1 reshape.205
  264.0 0.1 reshape.199
  264.1 0.0 copy-done
  264.1 0.2 fusion.58
  264.3 2.0 gather_fusion.1
  266.3 0.1 reshape.208
  266.5 0.1 copy.75
  266.6 0.1 copy.76
  266.7 75.3 %all-to-all-done.5 = bf16[32,16,1536]{2,1,0:T(8,128)(2,1)S(1)} async-done(((bf16[32,16,1536]{2,1,0:T(8,128)(2,1)}), bf16[32,16,1536]{2,1,0:T(8,128)(2,1)S(1)}, u32[]{:S(2)}, u32[]{:S(2)}) %all-to-all-start.5) | async-done | bytes 1572896 | tf_op jit(solution)/shard_map/all_to_all | solution.py:113
  342.0 1.3 gather_fusion
  343.2 1.0 reshape.215
  344.2 2.3 multiply_reduce_fusion.1
  346.5 0.8 fusion.33
  (17 shorter events, 0.3 us)
Async XLA Ops:
  6.5 257.6 %copy-start = (bf16[1536,32]{0,1:T(8,128)(2,1)S(1)}, bf16[1536,32]{0,1:T(8,128)(2,1)}, u32[]{:S(2)}) copy-start(bf16[1536,32]{0,1:T(8,128)(2,1)} %param.14) | copy-start | bytes 294916
  6.5 83.9 %copy-start.3 = (s32[1,1,128,2]{2,3,1,0:T(2,128)S(1)}, s32[1,1,128,2]{2,3,1,0:T(2,128)}, u32[]{:S(2)}) copy-start(s32[1,1,128,2]{2,3,1,0:T(2,128)} %param.17) | copy-start | bytes 3076
  6.5 240.4 %all-gather.5.cloned.1.call-start = ((), (), s32[]{:S(2)}) async-start(), calls=%async_computation.6 | async-start | bytes 6684672 | tf_op jit(solution)/shard_map/all_gather | solution.py:105
  85.5 32.3 %all-to-all-start.2 = ((bf16[32,3,16,128]{3,2,1,0:T(8,128)(2,1)}), bf16[32,3,16,128]{3,2,1,0:T(8,128)(2,1)S(1)}, u32[]{:S(2)}, u32[]{:S(2)}) async-start(bf16[32,3,16,128]{3,2,1,0:T(8,128)(2,1)} %bitcast.123), calls=%async_computation.2 | async-start | bytes 786432 | tf_op jit(solution)/shard_map/all_to_all | solution.py:62
  89.7 157.3 %all-gather.7.cloned.1.call-start = ((), (), s32[]{:S(2)}) async-start(), calls=%async_computation.7 | async-start | bytes 6684672 | tf_op jit(solution)/shard_map/all_gather | solution.py:106
  120.7 8.4 %copy-start.2 = (bf16[8,4,1536]{2,1,0:T(4,128)(2,1)S(1)}, bf16[8,4,1536]{2,1,0:T(4,128)(2,1)}, u32[]{:S(2)}) copy-start(bf16[8,4,1536]{2,1,0:T(4,128)(2,1)} %param.13) | copy-start | bytes 294916
  123.4 39.4 %copy-start.1 = (bf16[8,16,1536]{2,1,0:T(8,128)(2,1)S(1)}, bf16[8,16,1536]{2,1,0:T(8,128)(2,1)}, u32[]{:S(2)}) copy-start(bf16[8,16,1536]{2,1,0:T(8,128)(2,1)} %param.12) | copy-start | bytes 1179652
  124.6 38.0 %all-to-all-start.3 = ((bf16[1,3,512,128]{3,1,0,2:T(4,128)(2,1)}), bf16[1,3,512,128]{3,1,0,2:T(4,128)(2,1)S(1)}, u32[]{:S(2)}, u32[]{:S(2)}) async-start(bf16[1,3,512,128]{3,1,0,2:T(4,128)(2,1)} %copy.70), calls=%async_computation.3 | async-start | bytes 1048576 | tf_op jit(solution)/shard_map/all_to_all | solution.py:35
  259.5 82.5 %all-to-all-start.5 = ((bf16[32,16,1536]{2,1,0:T(8,128)(2,1)}), bf16[32,16,1536]{2,1,0:T(8,128)(2,1)S(1)}, u32[]{:S(2)}, u32[]{:S(2)}) async-start(bf16[32,16,1536]{2,1,0:T(8,128)(2,1)} %bitcast.115), calls=%async_computation.5 | async-start | bytes 3145728 | tf_op jit(solution)/shard_map/all_to_all | solution.py:113
Sparse Core Ops, SparseCore 0:
  9.5 56.2 all-gather.4
  92.7 53.0 all-gather.6
where the time goes:
time: 355 us; the launch traced here: 354 us
  blocking collectives  161 us (45%)
  waiting for transfers between devices  136 us (38%)
  matrix products  18.8 us (5%)
  between operations  13.7 us (4%)
  starting transfers between devices  12.7 us (4%)
  local copies, waits for them, and re-layouts  7.12 us (2%)
  other arithmetic  4.89 us (1%)
    all_to_all x1, blocking collectives, per_device(): lax.all_to_all(outbound, 'seq', split_axis=0, concat_axis=0, tiled=True)  82.8 us
    all_to_all x1, waiting for transfers between devices, per_device(): lax.all_to_all(results.reshape(group_indices, capacity, model_width), 'se...  75.3 us
    all_to_all x1, blocking collectives, per_device(): lax.all_to_all(arrange(query_heads), 'seq', split_axis=0, concat_axis=2,...  45.9 us
    all_to_all x1, waiting for transfers between devices, attend_items(): lax.all_to_all(merged, 'seq', split_axis=2, concat_axis=0, tiled=True)  33.4 us
    all_to_all x1, blocking collectives, per_device(): lax.all_to_all(arrange(key_heads), 'seq', split_axis=0, concat_axis=2, ti...  32.4 us
    all_to_all x1, waiting for transfers between devices, per_device(): lax.all_to_all(arrange(value_heads), 'seq', split_axis=0, concat_axis=2,...  25.9 us
    dot_general x1, matrix products, per_device(): summed = jnp.dot(hidden, down_piece, preferred_element_type=jnp.float32)  12.5 us
  transfers between devices with their start and end apart: 5, of which 3 were waited for; matrix products, arithmetic and copies ran while one was open for 4% of the time, Pallas kernels for 0%

commit v1 on v0

v1 whole, which is shorter than its diff:
```python
import math

import jax
import jax.numpy as jnp
from jax import lax
from jax.experimental import pallas as pl
from jax.experimental.pallas import tpu as pltpu
from jax.sharding import PartitionSpec as P

norm_eps = 1e-06
f32 = jnp.float32
bf16 = jnp.bfloat16


def attention_kernel(q_ref, k_ref, v_ref, o_ref):
    blocks, _, rows, width = q_ref.shape
    length = blocks * rows
    scale = 1.0 / math.sqrt(width)
    q = q_ref[...].reshape(length, width)
    k = k_ref[...].reshape(length, width)
    v = v_ref[...].reshape(length, width)
    scores = lax.dot_general(q, k, (((1,), (1,)), ((), ())), preferred_element_type=f32)
    top = jnp.max(scores, axis=1, keepdims=True)
    powers = jnp.exp((scores - top) * scale)
    total = jnp.sum(powers, axis=1, keepdims=True)
    weights = (powers * (1.0 / total)).astype(bf16)
    out = jnp.dot(weights, v, preferred_element_type=f32).astype(bf16)
    o_ref[...] = out.reshape(blocks, 1, rows, width)


def attend(qkv):
    blocks, triple, rows, width = qkv.shape
    pairs = triple // 3

    def spec(first):
        return pl.BlockSpec((blocks, 1, rows, width), lambda i: (0, first + i, 0, 0))

    length = blocks * rows
    return pl.pallas_call(
        attention_kernel,
        grid=(pairs,),
        in_specs=[spec(0), spec(pairs), spec(2 * pairs)],
        out_specs=spec(0),
        out_shape=jax.ShapeDtypeStruct((blocks, pairs, rows, width), bf16),
        compiler_params=pltpu.CompilerParams(vmem_limit_bytes=32 * 2**20),
        cost_estimate=pl.CostEstimate(
            flops=4 * pairs * length * length * width,
            bytes_accessed=8 * pairs * length * width,
            transcendentals=pairs * length * length,
        ),
        name="attend",
    )(qkv, qkv, qkv)


def choices(ids, experts):
    tokens = ids.shape[0]
    lanes = lax.broadcasted_iota(jnp.int32, (tokens, experts), 1)
    first = (lanes == ids[:, 0:1]).astype(f32)
    second = (lanes == ids[:, 1:2]).astype(f32)
    below = (
        lax.broadcasted_iota(jnp.int32, (tokens, tokens), 0)
        > lax.broadcasted_iota(jnp.int32, (tokens, tokens), 1)
    ).astype(bf16)
    before = jnp.dot(below, (first + second).astype(bf16), preferred_element_type=f32)
    capacity = 4 * tokens // experts
    out = []
    for k, onehot in enumerate((first, second)):
        slot = jnp.sum(before * onehot, axis=1, keepdims=True).astype(jnp.int32)
        out.append((onehot, ids[:, k : k + 1] * capacity + slot))
    return out


def placing(target, slots):
    tokens = target.shape[0]
    lanes = lax.broadcasted_iota(jnp.int32, (tokens, slots), 1)
    return (lanes == target).astype(f32).astype(bf16)


def route_kernel(attn_ref, res_ref, mod_ref, router_ref, ids_ref, stream_ref, out_ref, gate_ref, tok_ref):
    seqs, heads, rows, width = attn_ref.shape
    experts = router_ref.shape[1]
    for b in range(seqs):
        attn = jnp.concatenate([attn_ref[b, h].astype(f32) for h in range(heads)], axis=1)
        mod = mod_ref[b].astype(f32)
        stream = (res_ref[b].astype(f32) + mod[0:1] * attn).astype(bf16)
        stream_ref[b * rows : (b + 1) * rows, :] = stream
        wide = stream.astype(f32)
        center = jnp.mean(wide, axis=1, keepdims=True)
        moved = wide - center
        spread = jnp.mean(moved * moved, axis=1, keepdims=True)
        tok_ref[b * rows : (b + 1) * rows, :] = (
            moved * lax.rsqrt(spread + norm_eps) * mod[1:2] + mod[2:3]
        ).astype(bf16)
    tokens = tok_ref[...]
    logits = jnp.dot(tokens, router_ref[...], preferred_element_type=f32)
    picks = choices(ids_ref[...], experts)
    gates = [jax.nn.sigmoid(jnp.sum(onehot * logits, axis=1, keepdims=True)) for onehot, _ in picks]
    total = gates[0] + gates[1]
    gate_ref[...] = jnp.concatenate([gates[0] / total, gates[1] / total], axis=1)
    slots = out_ref.shape[0]
    place = placing(picks[0][1], slots) + placing(picks[1][1], slots)
    out_ref[...] = lax.dot_general(
        place, tokens, (((0,), (0,)), ((), ())), preferred_element_type=f32
    ).astype(bf16)


def route(attn, residual, modulation, router, ids):
    tokens = ids.shape[0]
    model_width = residual.shape[-1]
    slots = 4 * tokens
    return pl.pallas_call(
        route_kernel,
        out_shape=(
            jax.ShapeDtypeStruct((tokens, model_width), bf16),
            jax.ShapeDtypeStruct((slots, model_width), bf16),
            jax.ShapeDtypeStruct((tokens, 2), f32),
        ),
        scratch_shapes=[pltpu.VMEM((tokens, model_width), bf16)],
        compiler_params=pltpu.CompilerParams(vmem_limit_bytes=32 * 2**20),
        name="route",
    )(attn, residual, modulation, router, ids)


def combine_kernel(back_ref, stream_ref, mod_ref, gate_ref, ids_ref, out_ref, *, experts):
    seqs, rows, _ = out_ref.shape
    picks = choices(ids_ref[...], experts)
    slots = back_ref.shape[0]
    back = back_ref[...]
    moe = None
    for k in range(2):
        part = gate_ref[:, k : k + 1] * jnp.dot(
            placing(picks[k][1], slots), back, preferred_element_type=f32
        )
        moe = part if moe is None else moe + part
    for b in range(seqs):
        span = slice(b * rows, (b + 1) * rows)
        out_ref[b] = (
            stream_ref[span, :].astype(f32) + mod_ref[b, 3:4].astype(f32) * moe[span, :]
        ).astype(bf16)


def combine(back, stream, modulation, gates, ids, experts, rows):
    def kernel(*refs):
        combine_kernel(*refs, experts=experts)

    seqs = modulation.shape[0]
    return pl.pallas_call(
        kernel,
        out_shape=jax.ShapeDtypeStruct((seqs, rows, stream.shape[1]), bf16),
        compiler_params=pltpu.CompilerParams(vmem_limit_bytes=32 * 2**20),
        name="combine",
    )(back, stream, modulation, gates, ids)


def swap(blocks):
    return lax.all_to_all(blocks, "seq", split_axis=0, concat_axis=0, tiled=True)


def per_device(
    query_heads,
    key_heads,
    value_heads,
    residual,
    modulation,
    router,
    up_proj,
    down_proj,
    expert_ids,
):
    seqs_dev, head_count, len_dev, head_width = query_heads.shape
    group_indices = lax.axis_size("seq")
    pair_count = seqs_dev * head_count // group_indices
    tok_dev = seqs_dev * len_dev
    model_width = head_count * head_width
    experts = router.shape[1]
    capacity = 4 * tok_dev // experts
    ids = expert_ids.reshape(tok_dev, 2)

    up_piece = lax.all_gather(up_proj[0], "grp", axis=0, tiled=True)
    down_piece = lax.all_gather(down_proj[0], "grp", axis=0, tiled=True)

    def arrange(array):
        return array.reshape(group_indices, pair_count, len_dev, head_width)

    def together(*arrays):
        return swap(jnp.concatenate(arrays, axis=1))

    def apart(*arrays):
        return jnp.concatenate([swap(array) for array in arrays], axis=1)

    core = lax.axis_index("grp") % 2
    qkv = lax.cond(
        core == 0, together, apart, arrange(query_heads), arrange(key_heads), arrange(value_heads)
    )
    attn = swap(attend(qkv)).reshape(seqs_dev, head_count, len_dev, head_width)
    stream, outbound, gates = route(attn, residual, modulation, router, ids)
    arrived = swap(outbound.reshape(experts, capacity, model_width)).reshape(
        group_indices * capacity, model_width
    )
    pre_act = lax.dot_general(
        arrived, up_piece, (((1,), (1,)), ((), ())), preferred_element_type=f32
    )
    hidden = jax.nn.gelu(pre_act).astype(bf16)
    results = jnp.dot(hidden, down_piece, preferred_element_type=f32).astype(bf16)
    back = swap(results.reshape(group_indices, capacity, model_width)).reshape(
        experts * capacity, model_width
    )
    return combine(back, stream, modulation, gates, ids, experts, len_dev)


def solution(mesh):
    return jax.shard_map(
        per_device,
        mesh=mesh,
        in_specs=(
            P("grp", None, "seq", None),
            P("grp", None, "seq", None),
            P("grp", None, "seq", None),
            P("grp", "seq", None),
            P("grp", None, None),
            P(),
            P("seq", "grp", None),
            P("seq", "grp", None),
            P("grp", "seq", None, None),
        ),
        out_specs=P("grp", "seq", None),
        check_vma=False,
    )
```

time: 355 us -> 284 us (0.80)
  the two profiles are of different devices: /device:TPU:40 before, /device:TPU:1 now
where the time goes in v1:
time: 284 us; the launch traced here: 283 us
  blocking collectives  216 us (76%)
  waiting for transfers between devices  28.9 us (10%)
  between operations  13.5 us (5%)
  matrix products  12.5 us (4%)
  Pallas kernels  6.93 us (2%)
  starting transfers between devices  4.72 us (2%)
    all_to_all x5, blocking collectives, swap(): lax.all_to_all(blocks, 'seq', split_axis=0, concat_axis=0, tiled=True)  216 us
    all_to_all x1, waiting for transfers between devices, swap(): lax.all_to_all(blocks, 'seq', split_axis=0, concat_axis=0, tiled=True)  27.5 us
    dot_general x1, matrix products, per_device(): jnp.dot(hidden, down_piece, preferred_element_type=f32).astype(bf16)  12.5 us
  transfers between devices with their start and end apart: 3, of which 1 were waited for; matrix products, arithmetic and copies ran while one was open for 0% of the time, Pallas kernels for 2%

profile of v1, /device:TPU:1, one launch (start us, length us, event | category | flops | bytes accessed | tf_op | source)
XLA Modules:
  0.0 283.2 jit_solution(14725264012445579818)
XLA Ops:
  6.5 0.0 all-gather.5.cloned.1.call-start
  6.5 0.7 all-gather.5.cloned.1.call-update
  7.3 0.0 all-gather.7.cloned.1.call-start
  7.3 0.7 all-gather.7.cloned.1.call-update
  8.0 104.7 %conditional.1 = (bf16[32,9,16,128]{3,2,1,0:T(8,128)(2,1)S(1)}) conditional(s32[]{:T(128)} %convert_element_type.9, (bf16[32,3,16,128]{3,2,1,0:T(8,128)(2,1)}, bf16[32,3,16,128]{3,2,1,0:T(8,128)(2,1)}, bf16[32,3,16,128]{3,2,1,0:T(8,128)(2,1)}) %tuple.22, (bf16[32,3,16,128]{3,2,1,0:T(8,128)(2,1)}, bf16[32,3,16,128]{3,2,1,0:T(8,128)(2,1)}, ...), branch_computations={%region_0.1_spmd, %region_1.2_spmd} | conditional | flops 1179648 | bytes 4718600 | solution.py:192
  8.0 43.6 %all_to_all.31 = bf16[32,3,16,128]{3,2,1,0:T(8,128)(2,1)S(1)} all-to-all(bf16[32,3,16,128]{3,2,1,0:T(8,128)(2,1)} %get-tuple-element.20), channel_id=1, replica_groups=mesh['grp'=16,'seq'=32] {'seq'}, dimensions={0} | all-to-all | bytes 786432 | tf_op jit(solution)/shard_map/cond/branch_0_fun/all_to_all | solution.py:156
  51.7 29.7 %all_to_all.32 = bf16[32,3,16,128]{3,2,1,0:T(8,128)(2,1)S(1)} all-to-all(bf16[32,3,16,128]{3,2,1,0:T(8,128)(2,1)} %get-tuple-element.21), channel_id=1, replica_groups=mesh['grp'=16,'seq'=32] {'seq'}, dimensions={0} | all-to-all | bytes 786432 | tf_op jit(solution)/shard_map/cond/branch_0_fun/all_to_all | solution.py:156
  81.4 31.3 %all_to_all.33 = bf16[32,3,16,128]{3,2,1,0:T(8,128)(2,1)S(1)} all-to-all(bf16[32,3,16,128]{3,2,1,0:T(8,128)(2,1)} %get-tuple-element.22), channel_id=1, replica_groups=mesh['grp'=16,'seq'=32] {'seq'}, dimensions={0} | all-to-all | bytes 786432 | tf_op jit(solution)/shard_map/cond/branch_0_fun/all_to_all | solution.py:156
  112.6 0.1 pad_maximum_fusion
  112.8 0.0 copy-start.3
  112.8 0.0 copy-start.2
  112.8 0.0 copy-start
  112.8 0.0 copy-start.1
  112.8 3.7 %attend.1 = bf16[32,3,16,128]{3,2,1,0:T(8,128)(2,1)} custom-call(bf16[32,9,16,128]{3,2,1,0:T(8,128)(2,1)S(1)} %get-tuple-element.32.q_ref.k_ref.v_ref, bf16[32,9,16,128]{3,2,1,0:T(8,128)(2,1)S(1)} %get-tuple-element.32.q_ref.k_ref.v_ref, bf16[32,9,16,128]{3,2,1,0:T(8,128)(2,1)S(1)} %get-tuple-element.32.q_ref.k_ref.v_ref), custom_call_target="tpu_custom_call" | custom-call | flops 402653184 | bytes 1572864 | tf_op jit(solution)/shard_map/attend/pallas_call | solution.py:39
  116.5 4.7 %all-to-all-start.4 = ((bf16[32,3,16,128]{3,2,1,0:T(8,128)(2,1)}), bf16[32,3,16,128]{3,2,1,0:T(8,128)(2,1)S(1)}, u32[]{:S(2)}, u32[]{:S(2)}) async-start(bf16[32,3,16,128]{3,2,1,0:T(8,128)(2,1)} %attend.1), calls=%async_computation.4 | async-start | bytes 786432 | tf_op jit(solution)/shard_map/all_to_all | solution.py:156
  121.2 0.0 copy-done.3
  121.2 0.1 copy.10
  121.3 0.0 copy-done.2
  121.3 0.2 copy.11.router_ref
  121.5 27.5 %all-to-all-done.4 = bf16[32,3,16,128]{3,2,1,0:T(8,128)(2,1)S(1)} async-done(((bf16[32,3,16,128]{3,2,1,0:T(8,128)(2,1)}), bf16[32,3,16,128]{3,2,1,0:T(8,128)(2,1)S(1)}, u32[]{:S(2)}, u32[]{:S(2)}) %all-to-all-start.4) | async-done | bytes 393248 | tf_op jit(solution)/shard_map/all_to_all | solution.py:156
  149.0 0.0 copy-done
  149.0 0.0 copy-done.1
  149.0 1.5 route.1
  150.5 56.7 %all_to_all.35 = bf16[32,16,1536]{2,1,0:T(8,128)(2,1)S(1)} all-to-all(bf16[32,16,1536]{2,1,0:T(8,128)(2,1)S(1)} %bitcast.23), channel_id=1, replica_groups=mesh['grp'=16,'seq'=32] {'seq'}, dimensions={0} | all-to-all | bytes 3145728 | tf_op jit(solution)/shard_map/all_to_all | solution.py:156
  207.3 0.0 all-gather.5.cloned.1.call-done
  207.3 0.0 all-gather.7.cloned.1.call-done
  207.3 12.5 %fusion.12 = bf16[512,1536]{1,0:T(8,128)(2,1)} fusion(bf16[1,2048,1536]{2,1,0:T(8,128)(2,1)} %all-gather.7.cloned.1.call-done, bf16[512,1536]{1,0:T(8,128)(2,1)S(1)} %bitcast.27, bf16[1,2048,1536]{2,1,0:T(8,128)(2,1)} %all-gather.5.cloned.1.call-done), kind=kOutput, calls=%fused_computation.15 | convolution fusion | flops 6452674560 | bytes 15728640 | tf_op jit(solution)/shard_map/dot_general | solution.py:204
  219.8 54.9 %all_to_all.36 = bf16[32,16,1536]{2,1,0:T(8,128)(2,1)S(1)} all-to-all(bf16[32,16,1536]{2,1,0:T(8,128)(2,1)} %bitcast.28), channel_id=1, replica_groups=mesh['grp'=16,'seq'=32] {'seq'}, dimensions={0} | all-to-all | bytes 3145728 | tf_op jit(solution)/shard_map/all_to_all | solution.py:156
  274.6 1.7 combine.1
Async XLA Ops:
  6.5 200.7 %all-gather.5.cloned.1.call-start = ((), (), s32[]{:S(2)}) async-start(), calls=%async_computation.7 | async-start | bytes 6684672 | tf_op jit(solution)/shard_map/all_gather | solution.py:179
  7.3 200.0 %all-gather.7.cloned.1.call-start = ((), (), s32[]{:S(2)}) async-start(), calls=%async_computation.8 | async-start | bytes 6684672 | tf_op jit(solution)/shard_map/all_gather | solution.py:180
  112.8 8.4 %copy-start.3 = (s32[1,1,128,2]{2,3,1,0:T(2,128)S(1)}, s32[1,1,128,2]{2,3,1,0:T(2,128)}, u32[]{:S(2)}) copy-start(s32[1,1,128,2]{2,3,1,0:T(2,128)} %param.19) | copy-start | bytes 3076
  112.8 8.5 %copy-start.2 = (bf16[1536,32]{0,1:T(8,128)(2,1)S(1)}, bf16[1536,32]{0,1:T(8,128)(2,1)}, u32[]{:S(2)}) copy-start(bf16[1536,32]{0,1:T(8,128)(2,1)} %param.16) | copy-start | bytes 294916
  112.8 36.2 %copy-start = (bf16[8,4,1536]{2,1,0:T(4,128)(2,1)S(1)}, bf16[8,4,1536]{2,1,0:T(4,128)(2,1)}, u32[]{:S(2)}) copy-start(bf16[8,4,1536]{2,1,0:T(4,128)(2,1)} %refs_2_.1) | copy-start | bytes 294916
  112.8 36.2 %copy-start.1 = (bf16[8,16,1536]{2,1,0:T(8,128)(2,1)S(1)}, bf16[8,16,1536]{2,1,0:T(8,128)(2,1)}, u32[]{:S(2)}) copy-start(bf16[8,16,1536]{2,1,0:T(8,128)(2,1)} %res_ref.1) | copy-start | bytes 1179652
  116.5 32.5 %all-to-all-start.4 = ((bf16[32,3,16,128]{3,2,1,0:T(8,128)(2,1)}), bf16[32,3,16,128]{3,2,1,0:T(8,128)(2,1)S(1)}, u32[]{:S(2)}, u32[]{:S(2)}) async-start(bf16[32,3,16,128]{3,2,1,0:T(8,128)(2,1)} %attend.1), calls=%async_computation.4 | async-start | bytes 786432 | tf_op jit(solution)/shard_map/all_to_all | solution.py:156
Sparse Core Ops, SparseCore 0:
  9.5 64.3 all-gather.4
  76.0 54.8 all-gather.6

commit v2 on v1

--- a/solution.py
+++ b/solution.py
@@ -28,9 +28,8 @@
     o_ref[...] = out.reshape(blocks, 1, rows, width)
 
 
-def attend(qkv):
-    blocks, triple, rows, width = qkv.shape
-    pairs = triple // 3
+def attend(queries, query_first, others, key_first, value_first, pairs):
+    blocks, _, rows, width = queries.shape
 
     def spec(first):
         return pl.BlockSpec((blocks, 1, rows, width), lambda i: (0, first + i, 0, 0))
@@ -39,7 +38,7 @@
     return pl.pallas_call(
         attention_kernel,
         grid=(pairs,),
-        in_specs=[spec(0), spec(pairs), spec(2 * pairs)],
+        in_specs=[spec(query_first), spec(key_first), spec(value_first)],
         out_specs=spec(0),
         out_shape=jax.ShapeDtypeStruct((blocks, pairs, rows, width), bf16),
         compiler_params=pltpu.CompilerParams(vmem_limit_bytes=32 * 2**20),
@@ -49,11 +48,12 @@
             transcendentals=pairs * length * length,
         ),
         name="attend",
-    )(qkv, qkv, qkv)
+    )(queries, others, others)
 
 
 def choices(ids, experts):
-    tokens = ids.shape[0]
+    tokens = ids.shape[1]
+    ids = jnp.concatenate([ids.astype(f32), jnp.zeros((6, tokens), f32)], axis=0).T.astype(jnp.int32)
     lanes = lax.broadcasted_iota(jnp.int32, (tokens, experts), 1)
     first = (lanes == ids[:, 0:1]).astype(f32)
     second = (lanes == ids[:, 1:2]).astype(f32)
@@ -76,11 +76,21 @@
     return (lanes == target).astype(f32).astype(bf16)
 
 
-def route_kernel(attn_ref, res_ref, mod_ref, router_ref, ids_ref, stream_ref, out_ref, gate_ref, tok_ref):
-    seqs, heads, rows, width = attn_ref.shape
-    experts = router_ref.shape[1]
+def route_kernel(
+    first_ref, rest_ref, res_ref, mod_ref, router_ref, ids_ref, stream_ref, out_ref, gate_ref, tok_ref
+):
+    blocks, others, rows, width = rest_ref.shape
+    pairs = others + 1
+    seqs = mod_ref.shape[0]
+    heads = blocks * pairs // seqs
+
+    def attended(pair):
+        block, place = divmod(pair, pairs)
+        return (first_ref[block, 0] if place == 0 else rest_ref[block, place - 1]).astype(f32)
+
+    experts = router_ref.shape[0]
     for b in range(seqs):
-        attn = jnp.concatenate([attn_ref[b, h].astype(f32) for h in range(heads)], axis=1)
+        attn = jnp.concatenate([attended(b * heads + h) for h in range(heads)], axis=1)
         mod = mod_ref[b].astype(f32)
         stream = (res_ref[b].astype(f32) + mod[0:1] * attn).astype(bf16)
         stream_ref[b * rows : (b + 1) * rows, :] = stream
@@ -92,7 +102,9 @@
             moved * lax.rsqrt(spread + norm_eps) * mod[1:2] + mod[2:3]
         ).astype(bf16)
     tokens = tok_ref[...]
-    logits = jnp.dot(tokens, router_ref[...], preferred_element_type=f32)
+    logits = lax.dot_general(
+        tokens, router_ref[...], (((1,), (1,)), ((), ())), preferred_element_type=f32
+    )
     picks = choices(ids_ref[...], experts)
     gates = [jax.nn.sigmoid(jnp.sum(onehot * logits, axis=1, keepdims=True)) for onehot, _ in picks]
     total = gates[0] + gates[1]
@@ -104,8 +116,8 @@
     ).astype(bf16)
 
 
-def route(attn, residual, modulation, router, ids):
-    tokens = ids.shape[0]
+def route(first, rest, residual, modulation, router, ids):
+    tokens = ids.shape[1]
     model_width = residual.shape[-1]
     slots = 4 * tokens
     return pl.pallas_call(
@@ -118,7 +130,7 @@
         scratch_shapes=[pltpu.VMEM((tokens, model_width), bf16)],
         compiler_params=pltpu.CompilerParams(vmem_limit_bytes=32 * 2**20),
         name="route",
-    )(attn, residual, modulation, router, ids)
+    )(first, rest, residual, modulation, router, ids)
 
 
 def combine_kernel(back_ref, stream_ref, mod_ref, gate_ref, ids_ref, out_ref, *, experts):
@@ -174,7 +186,7 @@
     model_width = head_count * head_width
     experts = router.shape[1]
     capacity = 4 * tok_dev // experts
-    ids = expert_ids.reshape(tok_dev, 2)
+    ids = expert_ids.reshape(tok_dev, 2).T
 
     up_piece = lax.all_gather(up_proj[0], "grp", axis=0, tiled=True)
     down_piece = lax.all_gather(down_proj[0], "grp", axis=0, tiled=True)
@@ -182,18 +194,23 @@
     def arrange(array):
         return array.reshape(group_indices, pair_count, len_dev, head_width)
 
-    def together(*arrays):
-        return swap(jnp.concatenate(arrays, axis=1))
-
-    def apart(*arrays):
-        return jnp.concatenate([swap(array) for array in arrays], axis=1)
+    def whole(queries, keys, values):
+        qkv = swap(jnp.concatenate([queries, keys, values], axis=1))
+        back = swap(attend(qkv, 0, qkv, pair_count, 2 * pair_count, pair_count))
+        return back[:, :1], back[:, 1:]
+
+    def pieces(queries, keys, values):
+        head = swap(queries)
+        body = swap(jnp.concatenate([keys, values], axis=1))
+        rest = pair_count - 1
+        first = swap(attend(head, 0, body, 0, pair_count, 1))
+        return first, swap(attend(head, 1, body, 1, pair_count + 1, rest))
 
     core = lax.axis_index("grp") % 2
-    qkv = lax.cond(
-        core == 0, together, apart, arrange(query_heads), arrange(key_heads), arrange(value_heads)
-    )
-    attn = swap(attend(qkv)).reshape(seqs_dev, head_count, len_dev, head_width)
-    stream, outbound, gates = route(attn, residual, modulation, router, ids)
+    first, rest = lax.cond(
+        core == 0, whole, pieces, arrange(query_heads), arrange(key_heads), arrange(value_heads)
+    )
+    stream, outbound, gates = route(first, rest, residual, modulation, router.T, ids)
     arrived = swap(outbound.reshape(experts, capacity, model_width)).reshape(
         group_indices * capacity, model_width
     )

time: 284 us -> 278 us (0.979)
  blocking collectives: 216 us -> 180 us
  starting transfers between devices: 4.72 us -> 23.3 us
  waiting for transfers between devices: 28.9 us -> 39.4 us
    all_to_all x5 -> x4, blocking collectives: 216 us -> 180 us  [swap(): lax.all_to_all(blocks, 'seq', split_axis=0, concat_axis=0, tiled=True)]
    all_to_all x1 -> x2, starting transfers between devices: 4.68 us -> 23.2 us  [swap(): lax.all_to_all(blocks, 'seq', split_axis=0, concat_axis=0, tiled=True)]
    all_to_all x1 -> x2, waiting for transfers between devices: 27.5 us -> 38 us  [swap(): lax.all_to_all(blocks, 'seq', split_axis=0, concat_axis=0, tiled=True)]
  transfers between devices with their start and end apart: 3 -> 4, of which waited for: 1 -> 2; matrix products, arithmetic and copies ran while one was open for 0% -> 0% of each run, Pallas kernels for 2% -> 2%
where the time goes in v2:
time: 278 us; the launch traced here: 277 us
  blocking collectives  180 us (65%)
  waiting for transfers between devices  39.4 us (14%)
  starting transfers between devices  23.3 us (8%)
  between operations  13.5 us (5%)
  matrix products  12.6 us (5%)
  Pallas kernels  6.87 us (2%)
    all_to_all x4, blocking collectives, swap(): lax.all_to_all(blocks, 'seq', split_axis=0, concat_axis=0, tiled=True)  180 us
    all_to_all x2, waiting for transfers between devices, swap(): lax.all_to_all(blocks, 'seq', split_axis=0, concat_axis=0, tiled=True)  38 us
    all_to_all x2, starting transfers between devices, swap(): lax.all_to_all(blocks, 'seq', split_axis=0, concat_axis=0, tiled=True)  23.2 us
    dot_general x1, matrix products, per_device(): jnp.dot(hidden, down_piece, preferred_element_type=f32).astype(bf16)  12.6 us
  transfers between devices with their start and end apart: 4, of which 2 were waited for; matrix products, arithmetic and copies ran while one was open for 0% of the time, Pallas kernels for 2%

profile of v2, /device:TPU:1, one launch (start us, length us, event | category | flops | bytes accessed | tf_op | source)
XLA Modules:
  0.0 277.1 jit_solution(17403137046434367104)
XLA Ops:
  6.5 0.0 all-gather.5.cloned.1.call-start
  6.5 0.7 all-gather.5.cloned.1.call-update
  7.3 0.0 all-gather.7.cloned.1.call-start
  7.3 0.7 all-gather.7.cloned.1.call-update
  8.0 0.0 copy-start
  8.0 0.0 copy-start.1
  8.0 0.0 copy-start.2
  8.0 0.0 copy-start.3
  8.1 128.8 %conditional.1 = (bf16[32,1,16,128]{3,2,1,0:T(8,128)(2,1)S(1)}, bf16[32,2,16,128]{3,2,1,0:T(8,128)(2,1)S(1)}) conditional(s32[]{:T(128)} %convert_element_type.9, (bf16[32,3,16,128]{3,2,1,0:T(8,128)(2,1)}, bf16[32,3,16,128]{3,2,1,0:T(8,128)(2,1)}, bf16[32,3,16,128]{3,2,1,0:T(8,128)(2,1)}) %tuple.24, (bf16[32,3,16,128]{3,2,1,0:T(8,128)(2,1)}, ...), branch_computations={%region_0.1_spmd, %region_1.2_spmd} | conditional | flops 403832832 | bytes 7864336 | solution.py:210
  8.1 18.6 %all-to-all-start = ((bf16[32,3,16,128]{3,2,1,0:T(8,128)(2,1)}), bf16[32,3,16,128]{3,2,1,0:T(8,128)(2,1)S(1)}, u32[]{:S(2)}, u32[]{:S(2)}) async-start(bf16[32,3,16,128]{3,2,1,0:T(8,128)(2,1)} %get-tuple-element.17), calls=%async_computation | async-start | bytes 786432 | tf_op jit(solution)/shard_map/cond/branch_0_fun/all_to_all | solution.py:168
  26.7 1.2 pad_maximum_fusion
  27.9 24.1 %all-to-all-done.q_ref = bf16[32,3,16,128]{3,2,1,0:T(8,128)(2,1)S(1)} async-done(((bf16[32,3,16,128]{3,2,1,0:T(8,128)(2,1)}), bf16[32,3,16,128]{3,2,1,0:T(8,128)(2,1)S(1)}, u32[]{:S(2)}, u32[]{:S(2)}) %all-to-all-start) | async-done | bytes 393248 | tf_op jit(solution)/shard_map/cond/branch_0_fun/all_to_all | solution.py:168
  52.0 36.1 %all_to_all.34.k_ref.v_ref = bf16[32,6,16,128]{3,2,1,0:T(8,128)(2,1)S(1)} all-to-all(bf16[32,6,16,128]{3,2,1,0:T(8,128)(2,1)S(1)} %pad_maximum_fusion), channel_id=1, replica_groups=mesh['grp'=16,'seq'=32] {'seq'}, dimensions={0} | all-to-all | bytes 1572864 | tf_op jit(solution)/shard_map/cond/branch_0_fun/all_to_all | solution.py:168
  88.1 1.6 attend.3
  89.7 4.6 %all-to-all-start.2 = ((bf16[32,1,16,128]{3,2,1,0:T(8,128)(2,1)}), bf16[32,1,16,128]{3,2,1,0:T(8,128)(2,1)S(1)}, u32[]{:S(2)}, u32[]{:S(2)}) async-start(bf16[32,1,16,128]{3,2,1,0:T(8,128)(2,1)} %attend.3), calls=%async_computation.2 | async-start | bytes 262144 | tf_op jit(solution)/shard_map/cond/branch_0_fun/all_to_all | solution.py:168
  94.3 2.1 attend.4
  96.4 13.9 %all-to-all-done.2 = bf16[32,1,16,128]{3,2,1,0:T(8,128)(2,1)S(1)} async-done(((bf16[32,1,16,128]{3,2,1,0:T(8,128)(2,1)}), bf16[32,1,16,128]{3,2,1,0:T(8,128)(2,1)S(1)}, u32[]{:S(2)}, u32[]{:S(2)}) %all-to-all-start.2) | async-done | bytes 131104 | tf_op jit(solution)/shard_map/cond/branch_0_fun/all_to_all | solution.py:168
  110.3 26.5 %all_to_all.35 = bf16[32,2,16,128]{3,2,1,0:T(8,128)(2,1)S(1)} all-to-all(bf16[32,2,16,128]{3,2,1,0:T(8,128)(2,1)S(1)} %attend.4), channel_id=1, replica_groups=mesh['grp'=16,'seq'=32] {'seq'}, dimensions={0} | all-to-all | bytes 524288 | tf_op jit(solution)/shard_map/cond/branch_0_fun/all_to_all | solution.py:168
  136.8 0.0 copy-done
  136.8 0.0 copy-done.1
  136.8 0.0 copy-done.2
  136.8 0.0 copy-done.3
  136.9 1.3 route.1
  138.2 58.1 %all_to_all.38 = bf16[32,16,1536]{2,1,0:T(8,128)(2,1)S(1)} all-to-all(bf16[32,16,1536]{2,1,0:T(8,128)(2,1)S(1)} %bitcast.25), channel_id=1, replica_groups=mesh['grp'=16,'seq'=32] {'seq'}, dimensions={0} | all-to-all | bytes 3145728 | tf_op jit(solution)/shard_map/all_to_all | solution.py:168
  196.3 0.0 all-gather.5.cloned.1.call-done
  196.3 0.0 all-gather.7.cloned.1.call-done
  196.3 12.6 %fusion.12 = bf16[512,1536]{1,0:T(8,128)(2,1)} fusion(bf16[1,2048,1536]{2,1,0:T(8,128)(2,1)} %all-gather.7.cloned.1.call-done, bf16[512,1536]{1,0:T(8,128)(2,1)S(1)} %bitcast.29, bf16[1,2048,1536]{2,1,0:T(8,128)(2,1)} %all-gather.5.cloned.1.call-done), kind=kOutput, calls=%fused_computation.15 | convolution fusion | flops 6452674560 | bytes 15728640 | tf_op jit(solution)/shard_map/dot_general | solution.py:221
  208.9 59.5 %all_to_all.39 = bf16[32,16,1536]{2,1,0:T(8,128)(2,1)S(1)} all-to-all(bf16[32,16,1536]{2,1,0:T(8,128)(2,1)} %bitcast.30), channel_id=1, replica_groups=mesh['grp'=16,'seq'=32] {'seq'}, dimensions={0} | all-to-all | bytes 3145728 | tf_op jit(solution)/shard_map/all_to_all | solution.py:168
  268.4 1.9 combine.1
Async XLA Ops:
  6.5 189.8 %all-gather.5.cloned.1.call-start = ((), (), s32[]{:S(2)}) async-start(), calls=%async_computation.8 | async-start | bytes 6684672 | tf_op jit(solution)/shard_map/all_gather | solution.py:191
  7.3 189.0 %all-gather.7.cloned.1.call-start = ((), (), s32[]{:S(2)}) async-start(), calls=%async_computation.9 | async-start | bytes 6684672 | tf_op jit(solution)/shard_map/all_gather | solution.py:192
  8.0 128.8 %copy-start = (bf16[8,4,1536]{2,1,0:T(4,128)(2,1)S(1)}, bf16[8,4,1536]{2,1,0:T(4,128)(2,1)}, u32[]{:S(2)}) copy-start(bf16[8,4,1536]{2,1,0:T(4,128)(2,1)} %refs_2_.1) | copy-start | bytes 294916
  8.0 128.8 %copy-start.1 = (bf16[8,16,1536]{2,1,0:T(8,128)(2,1)S(1)}, bf16[8,16,1536]{2,1,0:T(8,128)(2,1)}, u32[]{:S(2)}) copy-start(bf16[8,16,1536]{2,1,0:T(8,128)(2,1)} %res_ref.1) | copy-start | bytes 1179652
  8.0 128.8 %copy-start.2 = (bf16[1536,32]{0,1:T(8,128)(2,1)S(1)}, bf16[1536,32]{0,1:T(8,128)(2,1)}, u32[]{:S(2)}) copy-start(bf16[1536,32]{0,1:T(8,128)(2,1)} %param.16) | copy-start | bytes 294916
  8.0 128.8 %copy-start.3 = (s32[1,1,128,2]{2,3,1,0:T(2,128)S(1)}, s32[1,1,128,2]{2,3,1,0:T(2,128)}, u32[]{:S(2)}) copy-start(s32[1,1,128,2]{2,3,1,0:T(2,128)} %param.19) | copy-start | bytes 3076
  8.1 43.9 %all-to-all-start = ((bf16[32,3,16,128]{3,2,1,0:T(8,128)(2,1)}), bf16[32,3,16,128]{3,2,1,0:T(8,128)(2,1)S(1)}, u32[]{:S(2)}, u32[]{:S(2)}) async-start(bf16[32,3,16,128]{3,2,1,0:T(8,128)(2,1)} %get-tuple-element.17), calls=%async_computation | async-start | bytes 786432 | tf_op jit(solution)/shard_map/cond/branch_0_fun/all_to_all | solution.py:168
  89.7 20.6 %all-to-all-start.2 = ((bf16[32,1,16,128]{3,2,1,0:T(8,128)(2,1)}), bf16[32,1,16,128]{3,2,1,0:T(8,128)(2,1)S(1)}, u32[]{:S(2)}, u32[]{:S(2)}) async-start(bf16[32,1,16,128]{3,2,1,0:T(8,128)(2,1)} %attend.3), calls=%async_computation.2 | async-start | bytes 262144 | tf_op jit(solution)/shard_map/cond/branch_0_fun/all_to_all | solution.py:168
Sparse Core Ops, SparseCore 0:
  9.5 64.7 all-gather.4
  76.4 55.5 all-gather.6

commit v3 on v1

--- a/solution.py
+++ b/solution.py
@@ -152,6 +152,64 @@
     )(back, stream, modulation, gates, ids)
 
 
+def mlp_kernel(x_ref, up_ref, down_ref, o_ref, pre_ref, acc_ref):
+    step = pl.program_id(0)
+    last = pl.num_programs(0) - 1
+
+    def ahead():
+        return lax.dot_general(
+            x_ref[...], up_ref[...], (((1,), (1,)), ((), ())), preferred_element_type=f32
+        )
+
+    def behind():
+        hidden = jax.nn.gelu(pre_ref[...]).astype(bf16)
+        return jnp.dot(hidden, down_ref[...], preferred_element_type=f32)
+
+    @pl.when(step == 0)
+    def _():
+        pre_ref[...] = ahead()
+
+    @pl.when(step == 1)
+    def _():
+        part, pre = behind(), ahead()
+        acc_ref[...] = part
+        pre_ref[...] = pre
+
+    @pl.when((step > 1) & (step < last))
+    def _():
+        part, pre = behind(), ahead()
+        acc_ref[...] += part
+        pre_ref[...] = pre
+
+    @pl.when(step == last)
+    def _():
+        o_ref[...] = (acc_ref[...] + behind()).astype(bf16)
+
+
+def mlp(rows, up, down, tile):
+    count, width = rows.shape
+    tiles = up.shape[0] // tile
+    return pl.pallas_call(
+        mlp_kernel,
+        grid=(tiles + 1,),
+        in_specs=[
+            pl.BlockSpec((count, width), lambda i: (0, 0)),
+            pl.BlockSpec((tile, width), lambda i: (jnp.minimum(i, tiles - 1), 0)),
+            pl.BlockSpec((tile, width), lambda i: (jnp.maximum(i - 1, 0), 0)),
+        ],
+        out_specs=pl.BlockSpec((count, width), lambda i: (0, 0)),
+        out_shape=jax.ShapeDtypeStruct((count, width), bf16),
+        scratch_shapes=[pltpu.VMEM((count, tile), f32), pltpu.VMEM((count, width), f32)],
+        compiler_params=pltpu.CompilerParams(vmem_limit_bytes=46 * 2**20),
+        cost_estimate=pl.CostEstimate(
+            flops=4 * count * width * up.shape[0],
+            bytes_accessed=4 * width * (count + up.shape[0]),
+            transcendentals=count * up.shape[0],
+        ),
+        name="mlp",
+    )(rows, up, down)
+
+
 def swap(blocks):
     return lax.all_to_all(blocks, "seq", split_axis=0, concat_axis=0, tiled=True)
 
@@ -186,22 +244,24 @@
         return swap(jnp.concatenate(arrays, axis=1))
 
     def apart(*arrays):
-        return jnp.concatenate([swap(array) for array in arrays], axis=1)
+        parts = [swap(arrays[0]), swap(jnp.concatenate(arrays[1:], axis=1))]
+        return jnp.concatenate(parts, axis=1)
 
     core = lax.axis_index("grp") % 2
     qkv = lax.cond(
         core == 0, together, apart, arrange(query_heads), arrange(key_heads), arrange(value_heads)
     )
-    attn = swap(attend(qkv)).reshape(seqs_dev, head_count, len_dev, head_width)
+    def by_pair(pairs):
+        return jnp.concatenate([swap(pairs[:, :1]), swap(pairs[:, 1:])], axis=1)
+
+    attn = lax.cond(core == 0, swap, by_pair, attend(qkv)).reshape(
+        seqs_dev, head_count, len_dev, head_width
+    )
     stream, outbound, gates = route(attn, residual, modulation, router, ids)
     arrived = swap(outbound.reshape(experts, capacity, model_width)).reshape(
         group_indices * capacity, model_width
     )
-    pre_act = lax.dot_general(
-        arrived, up_piece, (((1,), (1,)), ((), ())), preferred_element_type=f32
-    )
-    hidden = jax.nn.gelu(pre_act).astype(bf16)
-    results = jnp.dot(hidden, down_piece, preferred_element_type=f32).astype(bf16)
+    results = mlp(arrived, up_piece, down_piece, 4 * up_proj.shape[1])
     back = swap(results.reshape(group_indices, capacity, model_width)).reshape(
         experts * capacity, model_width
     )

time: 284 us -> 272 us (0.958)
  blocking collectives: 216 us -> 175 us
  starting transfers between devices: 4.72 us -> 23.2 us
  matrix products: 12.5 us -> 0 us
  waiting for transfers between devices: 28.9 us -> 41.2 us
  Pallas kernels: 6.93 us -> 16.1 us
    all_to_all x5 -> x4, blocking collectives: 216 us -> 175 us  [swap(): lax.all_to_all(blocks, 'seq', split_axis=0, concat_axis=0, tiled=True)]
    all_to_all x1 -> x2, starting transfers between devices: 4.68 us -> 23.1 us  [swap(): lax.all_to_all(blocks, 'seq', split_axis=0, concat_axis=0, tiled=True)]
    dot_general x1 -> x0, matrix products: 12.5 us -> none  [per_device(): jnp.dot(hidden, down_piece, preferred_element_type=f32).astype(bf16)]
    all_to_all x1 -> x2, waiting for transfers between devices: 27.5 us -> 39.8 us  [swap(): lax.all_to_all(blocks, 'seq', split_axis=0, concat_axis=0, tiled=True)]
    pallas_call x0 -> x1, Pallas kernels: none -> 9.76 us  [mlp(): pl.pallas_call(mlp_kernel, grid=(tiles + 1,), in_specs=[pl.BlockSpec((cou...]
  transfers between devices with their start and end apart: 3 -> 4, of which waited for: 1 -> 2; matrix products, arithmetic and copies ran while one was open for 0% -> 1% of each run, Pallas kernels for 2% -> 2%
where the time goes in v3:
time: 272 us
  blocking collectives  175 us (64%)
  waiting for transfers between devices  41.2 us (15%)
  starting transfers between devices  23.2 us (9%)
  Pallas kernels  16.1 us (6%)
  between operations  13.5 us (5%)
    all_to_all x4, blocking collectives, swap(): lax.all_to_all(blocks, 'seq', split_axis=0, concat_axis=0, tiled=True)  175 us
    all_to_all x2, waiting for transfers between devices, swap(): lax.all_to_all(blocks, 'seq', split_axis=0, concat_axis=0, tiled=True)  39.8 us
    all_to_all x2, starting transfers between devices, swap(): lax.all_to_all(blocks, 'seq', split_axis=0, concat_axis=0, tiled=True)  23.1 us
    pallas_call x1, Pallas kernels, mlp(): pl.pallas_call(mlp_kernel, grid=(tiles + 1,), in_specs=[pl.BlockSpec((cou...  9.76 us
  transfers between devices with their start and end apart: 4, of which 2 were waited for; matrix products, arithmetic and copies ran while one was open for 1% of the time, Pallas kernels for 2%

profile of v3, /device:TPU:1, one launch (start us, length us, event | category | flops | bytes accessed | tf_op | source)
XLA Modules:
  0.0 271.8 jit_solution(16885080877899166917)
XLA Ops:
  6.5 0.0 all-gather.5.cloned.1.call-start
  6.5 0.7 all-gather.5.cloned.1.call-update
  7.3 0.0 all-gather.7.cloned.1.call-start
  7.3 0.7 all-gather.7.cloned.1.call-update
  8.0 80.0 %conditional.2 = (bf16[32,9,16,128]{3,2,1,0:T(8,128)(2,1)S(1)}) conditional(s32[]{:T(128)} %convert_element_type.4, (bf16[32,3,16,128]{3,2,1,0:T(8,128)(2,1)}, bf16[32,3,16,128]{3,2,1,0:T(8,128)(2,1)}, bf16[32,3,16,128]{3,2,1,0:T(8,128)(2,1)}) %tuple.32, (bf16[32,3,16,128]{3,2,1,0:T(8,128)(2,1)}, bf16[32,3,16,128]{3,2,1,0:T(8,128)(2,1)}, ...), branch_computations={%region_0.1_spmd, %region_1.2_spmd} | conditional | flops 1179648 | bytes 6684712 | solution.py:251
  8.0 18.5 %all-to-all-start.1 = ((bf16[32,3,16,128]{3,2,1,0:T(8,128)(2,1)}), bf16[32,3,16,128]{3,2,1,0:T(8,128)(2,1)S(1)}, u32[]{:S(2)}, u32[]{:S(2)}) async-start(bf16[32,3,16,128]{3,2,1,0:T(8,128)(2,1)} %get-tuple-element.26), calls=%async_computation.1 | async-start | bytes 786432 | tf_op jit(solution)/shard_map/cond/branch_0_fun/all_to_all | solution.py:214
  26.5 1.2 pad_maximum_fusion.1
  27.7 23.9 %all-to-all-done.1 = bf16[32,3,16,128]{3,2,1,0:T(8,128)(2,1)S(1)} async-done(((bf16[32,3,16,128]{3,2,1,0:T(8,128)(2,1)}), bf16[32,3,16,128]{3,2,1,0:T(8,128)(2,1)S(1)}, u32[]{:S(2)}, u32[]{:S(2)}) %all-to-all-start.1) | async-done | bytes 393248 | tf_op jit(solution)/shard_map/cond/branch_0_fun/all_to_all | solution.py:214
  51.7 36.2 %all_to_all.34 = bf16[32,6,16,128]{3,2,1,0:T(8,128)(2,1)S(1)} all-to-all(bf16[32,6,16,128]{3,2,1,0:T(8,128)(2,1)S(1)} %pad_maximum_fusion.1), channel_id=1, replica_groups=mesh['grp'=16,'seq'=32] {'seq'}, dimensions={0} | all-to-all | bytes 1572864 | tf_op jit(solution)/shard_map/cond/branch_0_fun/all_to_all | solution.py:214
  87.9 0.1 pad_maximum_fusion
  88.0 3.1 %attend.1 = bf16[32,3,16,128]{3,2,1,0:T(8,128)(2,1)S(1)} custom-call(bf16[32,9,16,128]{3,2,1,0:T(8,128)(2,1)S(1)} %get-tuple-element.38.q_ref.k_ref.v_ref, bf16[32,9,16,128]{3,2,1,0:T(8,128)(2,1)S(1)} %get-tuple-element.38.q_ref.k_ref.v_ref, bf16[32,9,16,128]{3,2,1,0:T(8,128)(2,1)S(1)} %get-tuple-element.38.q_ref.k_ref.v_ref), custom_call_target="tpu_custom_call" | custom-call | flops 402653184 | bytes 1572864 | tf_op jit(solution)/shard_map/attend/pallas_call | solution.py:39
  91.1 0.0 copy-start.3
  91.1 0.0 copy-start.2
  91.1 0.0 copy-start
  91.1 0.0 copy-start.1
  91.2 46.3 %conditional.3 = (bf16[8,12,16,128]{3,2,1,0:T(8,128)(2,1)S(1)}) conditional(s32[]{:T(128)} %convert_element_type.4, bf16[32,3,16,128]{3,2,1,0:T(8,128)(2,1)S(1)} %attend.1, bf16[32,3,16,128]{3,2,1,0:T(8,128)(2,1)S(1)} %attend.1), branch_computations={%region_2.3_spmd, %region_3.4_spmd} | conditional | flops 196608 | bytes 2490408 | solution.py:257
  91.2 0.7 slice.4
  91.8 4.6 %all-to-all-start.4 = ((bf16[32,1,16,128]{3,2,1,0:T(8,128)(2,1)}), bf16[32,1,16,128]{3,2,1,0:T(8,128)(2,1)S(1)}, u32[]{:S(2)}, u32[]{:S(2)}) async-start(bf16[32,1,16,128]{3,2,1,0:T(8,128)(2,1)} %slice.4), calls=%async_computation.4 | async-start | bytes 262144 | tf_op jit(solution)/shard_map/cond/branch_0_fun/all_to_all | solution.py:214
  96.5 15.9 %all-to-all-done.4 = bf16[32,1,16,128]{3,2,1,0:T(8,128)(2,1)S(1)} async-done(((bf16[32,1,16,128]{3,2,1,0:T(8,128)(2,1)}), bf16[32,1,16,128]{3,2,1,0:T(8,128)(2,1)S(1)}, u32[]{:S(2)}, u32[]{:S(2)}) %all-to-all-start.4) | async-done | bytes 131104 | tf_op jit(solution)/shard_map/cond/branch_0_fun/all_to_all | solution.py:214
  112.4 25.1 %all_to_all.36 = bf16[32,2,16,128]{3,2,1,0:T(8,128)(2,1)S(1)} all-to-all(bf16[32,2,16,128]{3,2,1,0:T(8,128)(2,1)S(1)} %slice.5), channel_id=1, replica_groups=mesh['grp'=16,'seq'=32] {'seq'}, dimensions={0} | all-to-all | bytes 524288 | tf_op jit(solution)/shard_map/cond/branch_0_fun/all_to_all | solution.py:214
  137.5 0.0 copy-done.3
  137.5 0.1 copy.10
  137.6 0.0 copy-done.2
  137.6 0.2 copy.11.router_ref
  137.8 0.0 copy-done
  137.9 0.0 copy-done.1
  137.9 1.5 route.1
  139.4 57.0 %all_to_all.38 = bf16[32,16,1536]{2,1,0:T(8,128)(2,1)S(1)} all-to-all(bf16[32,16,1536]{2,1,0:T(8,128)(2,1)S(1)} %bitcast.14), channel_id=1, replica_groups=mesh['grp'=16,'seq'=32] {'seq'}, dimensions={0} | all-to-all | bytes 3145728 | tf_op jit(solution)/shard_map/all_to_all | solution.py:214
  196.4 0.0 all-gather.5.cloned.1.call-done
  196.4 0.0 all-gather.7.cloned.1.call-done
  196.4 9.8 %mlp.1 = bf16[512,1536]{1,0:T(8,128)(2,1)S(1)} custom-call(bf16[512,1536]{1,0:T(8,128)(2,1)S(1)} %bitcast.13, bf16[2048,1536]{1,0:T(8,128)(2,1)} %bitcast.26, bf16[2048,1536]{1,0:T(8,128)(2,1)} %bitcast.27), custom_call_target="tpu_custom_call" | custom-call | flops 6442450944 | bytes 15728640 | tf_op jit(solution)/shard_map/mlp/pallas_call | solution.py:192
  206.2 57.0 %all_to_all.39 = bf16[32,16,1536]{2,1,0:T(8,128)(2,1)S(1)} all-to-all(bf16[32,16,1536]{2,1,0:T(8,128)(2,1)S(1)} %bitcast.15), channel_id=1, replica_groups=mesh['grp'=16,'seq'=32] {'seq'}, dimensions={0} | all-to-all | bytes 3145728 | tf_op jit(solution)/shard_map/all_to_all | solution.py:214
  263.2 1.7 combine.1
  (2 shorter events, 0.1 us)
Async XLA Ops:
  6.5 189.9 %all-gather.5.cloned.1.call-start = ((), (), s32[]{:S(2)}) async-start(), calls=%async_computation.8 | async-start | bytes 6684672 | tf_op jit(solution)/shard_map/all_gather | solution.py:237
  7.3 189.2 %all-gather.7.cloned.1.call-start = ((), (), s32[]{:S(2)}) async-start(), calls=%async_computation.9 | async-start | bytes 6684672 | tf_op jit(solution)/shard_map/all_gather | solution.py:238
  8.0 43.7 %all-to-all-start.1 = ((bf16[32,3,16,128]{3,2,1,0:T(8,128)(2,1)}), bf16[32,3,16,128]{3,2,1,0:T(8,128)(2,1)S(1)}, u32[]{:S(2)}, u32[]{:S(2)}) async-start(bf16[32,3,16,128]{3,2,1,0:T(8,128)(2,1)} %get-tuple-element.26), calls=%async_computation.1 | async-start | bytes 786432 | tf_op jit(solution)/shard_map/cond/branch_0_fun/all_to_all | solution.py:214
  91.1 46.4 %copy-start.3 = (s32[1,1,128,2]{2,3,1,0:T(2,128)S(1)}, s32[1,1,128,2]{2,3,1,0:T(2,128)}, u32[]{:S(2)}) copy-start(s32[1,1,128,2]{2,3,1,0:T(2,128)} %param.21) | copy-start | bytes 3076
  91.1 46.5 %copy-start.2 = (bf16[1536,32]{0,1:T(8,128)(2,1)S(1)}, bf16[1536,32]{0,1:T(8,128)(2,1)}, u32[]{:S(2)}) copy-start(bf16[1536,32]{0,1:T(8,128)(2,1)} %param.18) | copy-start | bytes 294916
  91.1 46.7 %copy-start = (bf16[8,4,1536]{2,1,0:T(4,128)(2,1)S(1)}, bf16[8,4,1536]{2,1,0:T(4,128)(2,1)}, u32[]{:S(2)}) copy-start(bf16[8,4,1536]{2,1,0:T(4,128)(2,1)} %refs_2_.1) | copy-start | bytes 294916
  91.1 46.7 %copy-start.1 = (bf16[8,16,1536]{2,1,0:T(8,128)(2,1)S(1)}, bf16[8,16,1536]{2,1,0:T(8,128)(2,1)}, u32[]{:S(2)}) copy-start(bf16[8,16,1536]{2,1,0:T(8,128)(2,1)} %res_ref.1) | copy-start | bytes 1179652
  91.8 20.5 %all-to-all-start.4 = ((bf16[32,1,16,128]{3,2,1,0:T(8,128)(2,1)}), bf16[32,1,16,128]{3,2,1,0:T(8,128)(2,1)S(1)}, u32[]{:S(2)}, u32[]{:S(2)}) async-start(bf16[32,1,16,128]{3,2,1,0:T(8,128)(2,1)} %slice.4), calls=%async_computation.4 | async-start | bytes 262144 | tf_op jit(solution)/shard_map/cond/branch_0_fun/all_to_all | solution.py:214
Sparse Core Ops, SparseCore 0:
  9.5 64.5 all-gather.4
  76.3 56.1 all-gather.6

commit v4 on v3

--- a/solution.py
+++ b/solution.py
@@ -12,35 +12,26 @@
 bf16 = jnp.bfloat16
 
 
-def attention_kernel(q_ref, k_ref, v_ref, o_ref):
-    blocks, _, rows, width = q_ref.shape
+def attention_kernel(qkv_ref, o_ref):
+    blocks, pairs, rows, width = o_ref.shape
     length = blocks * rows
     scale = 1.0 / math.sqrt(width)
-    q = q_ref[...].reshape(length, width)
-    k = k_ref[...].reshape(length, width)
-    v = v_ref[...].reshape(length, width)
-    scores = lax.dot_general(q, k, (((1,), (1,)), ((), ())), preferred_element_type=f32)
-    top = jnp.max(scores, axis=1, keepdims=True)
-    powers = jnp.exp((scores - top) * scale)
-    total = jnp.sum(powers, axis=1, keepdims=True)
-    weights = (powers * (1.0 / total)).astype(bf16)
-    out = jnp.dot(weights, v, preferred_element_type=f32).astype(bf16)
-    o_ref[...] = out.reshape(blocks, 1, rows, width)
+    for i in range(pairs):
+        q, k, v = (qkv_ref[:, i + kind * pairs].reshape(length, width) for kind in range(3))
+        scores = lax.dot_general(q, k, (((1,), (1,)), ((), ())), preferred_element_type=f32)
+        top = jnp.max(scores, axis=1, keepdims=True)
+        powers = jnp.exp((scores - top) * scale)
+        total = jnp.sum(powers, axis=1, keepdims=True)
+        out = jnp.dot(powers.astype(bf16), v, preferred_element_type=f32) * (1.0 / total)
+        o_ref[:, i] = out.astype(bf16).reshape(blocks, rows, width)
 
 
 def attend(qkv):
     blocks, triple, rows, width = qkv.shape
     pairs = triple // 3
-
-    def spec(first):
-        return pl.BlockSpec((blocks, 1, rows, width), lambda i: (0, first + i, 0, 0))
-
     length = blocks * rows
     return pl.pallas_call(
         attention_kernel,
-        grid=(pairs,),
-        in_specs=[spec(0), spec(pairs), spec(2 * pairs)],
-        out_specs=spec(0),
         out_shape=jax.ShapeDtypeStruct((blocks, pairs, rows, width), bf16),
         compiler_params=pltpu.CompilerParams(vmem_limit_bytes=32 * 2**20),
         cost_estimate=pl.CostEstimate(
@@ -49,7 +40,7 @@
             transcendentals=pairs * length * length,
         ),
         name="attend",
-    )(qkv, qkv, qkv)
+    )(qkv)
 
 
 def choices(ids, experts):
@@ -126,12 +117,10 @@
     picks = choices(ids_ref[...], experts)
     slots = back_ref.shape[0]
     back = back_ref[...]
-    moe = None
-    for k in range(2):
-        part = gate_ref[:, k : k + 1] * jnp.dot(
-            placing(picks[k][1], slots), back, preferred_element_type=f32
-        )
-        moe = part if moe is None else moe + part
+    tokens = stream_ref.shape[0]
+    place = jnp.concatenate([placing(target, slots) for _, target in picks], axis=0)
+    fetched = jnp.dot(place, back, preferred_element_type=f32)
+    moe = gate_ref[:, 0:1] * fetched[:tokens] + gate_ref[:, 1:2] * fetched[tokens:]
     for b in range(seqs):
         span = slice(b * rows, (b + 1) * rows)
         out_ref[b] = (

time: 272 us -> 271 us (level)
  transfers between devices with their start and end apart: 4 -> 4, of which waited for: 2 -> 2; matrix products, arithmetic and copies ran while one was open for 1% -> 1% of each run, Pallas kernels for 2% -> 1%
where the time goes in v4:
time: 271 us; the launch traced here: 270 us
  blocking collectives  175 us (65%)
  waiting for transfers between devices  41.2 us (15%)
  starting transfers between devices  23.2 us (9%)
  Pallas kernels  14.5 us (5%)
  between operations  13.5 us (5%)
    all_to_all x4, blocking collectives, swap(): lax.all_to_all(blocks, 'seq', split_axis=0, concat_axis=0, tiled=True)  175 us
    all_to_all x2, waiting for transfers between devices, swap(): lax.all_to_all(blocks, 'seq', split_axis=0, concat_axis=0, tiled=True)  39.8 us
    all_to_all x2, starting transfers between devices, swap(): lax.all_to_all(blocks, 'seq', split_axis=0, concat_axis=0, tiled=True)  23.1 us
    pallas_call x1, Pallas kernels, mlp(): pl.pallas_call(mlp_kernel, grid=(tiles + 1,), in_specs=[pl.BlockSpec((cou...  9.76 us
  transfers between devices with their start and end apart: 4, of which 2 were waited for; matrix products, arithmetic and copies ran while one was open for 1% of the time, Pallas kernels for 1%

profile of v4, /device:TPU:1, one launch (start us, length us, event | category | flops | bytes accessed | tf_op | source)
XLA Modules:
  0.0 270.3 jit_solution(5316673058530370064)
XLA Ops:
  6.5 0.0 all-gather.5.cloned.1.call-start
  6.5 0.7 all-gather.5.cloned.1.call-update
  7.3 0.0 all-gather.7.cloned.1.call-start
  7.3 0.7 all-gather.7.cloned.1.call-update
  8.0 80.0 %conditional.2 = (bf16[32,9,16,128]{3,2,1,0:T(8,128)(2,1)S(1)}) conditional(s32[]{:T(128)} %convert_element_type.4, (bf16[32,3,16,128]{3,2,1,0:T(8,128)(2,1)}, bf16[32,3,16,128]{3,2,1,0:T(8,128)(2,1)}, bf16[32,3,16,128]{3,2,1,0:T(8,128)(2,1)}) %tuple.32, (bf16[32,3,16,128]{3,2,1,0:T(8,128)(2,1)}, bf16[32,3,16,128]{3,2,1,0:T(8,128)(2,1)}, ...), branch_computations={%region_0.1_spmd, %region_1.2_spmd} | conditional | flops 1179648 | bytes 6684712 | solution.py:240
  8.0 18.5 %all-to-all-start.1 = ((bf16[32,3,16,128]{3,2,1,0:T(8,128)(2,1)}), bf16[32,3,16,128]{3,2,1,0:T(8,128)(2,1)S(1)}, u32[]{:S(2)}, u32[]{:S(2)}) async-start(bf16[32,3,16,128]{3,2,1,0:T(8,128)(2,1)} %get-tuple-element.26), calls=%async_computation.1 | async-start | bytes 786432 | tf_op jit(solution)/shard_map/cond/branch_0_fun/all_to_all | solution.py:203
  26.5 1.2 pad_maximum_fusion.1
  27.7 23.9 %all-to-all-done.1 = bf16[32,3,16,128]{3,2,1,0:T(8,128)(2,1)S(1)} async-done(((bf16[32,3,16,128]{3,2,1,0:T(8,128)(2,1)}), bf16[32,3,16,128]{3,2,1,0:T(8,128)(2,1)S(1)}, u32[]{:S(2)}, u32[]{:S(2)}) %all-to-all-start.1) | async-done | bytes 393248 | tf_op jit(solution)/shard_map/cond/branch_0_fun/all_to_all | solution.py:203
  51.7 36.2 %all_to_all.34 = bf16[32,6,16,128]{3,2,1,0:T(8,128)(2,1)S(1)} all-to-all(bf16[32,6,16,128]{3,2,1,0:T(8,128)(2,1)S(1)} %pad_maximum_fusion.1), channel_id=1, replica_groups=mesh['grp'=16,'seq'=32] {'seq'}, dimensions={0} | all-to-all | bytes 1572864 | tf_op jit(solution)/shard_map/cond/branch_0_fun/all_to_all | solution.py:203
  87.9 0.1 pad_maximum_fusion
  88.0 1.4 attend.1
  89.4 0.0 copy-start.3
  89.4 0.0 copy-start.2
  89.5 0.0 copy-start
  89.5 0.0 copy-start.1
  89.5 46.4 %conditional.3 = (bf16[8,12,16,128]{3,2,1,0:T(8,128)(2,1)S(1)}) conditional(s32[]{:T(128)} %convert_element_type.4, bf16[32,3,16,128]{3,2,1,0:T(8,128)(2,1)S(1)} %attend.1, bf16[32,3,16,128]{3,2,1,0:T(8,128)(2,1)S(1)} %attend.1), branch_computations={%region_2.3_spmd, %region_3.4_spmd} | conditional | flops 196608 | bytes 2490408 | solution.py:246
  89.5 0.7 slice.4
  90.2 4.6 %all-to-all-start.4 = ((bf16[32,1,16,128]{3,2,1,0:T(8,128)(2,1)}), bf16[32,1,16,128]{3,2,1,0:T(8,128)(2,1)S(1)}, u32[]{:S(2)}, u32[]{:S(2)}) async-start(bf16[32,1,16,128]{3,2,1,0:T(8,128)(2,1)} %slice.4), calls=%async_computation.4 | async-start | bytes 262144 | tf_op jit(solution)/shard_map/cond/branch_0_fun/all_to_all | solution.py:203
  94.8 15.9 %all-to-all-done.4 = bf16[32,1,16,128]{3,2,1,0:T(8,128)(2,1)S(1)} async-done(((bf16[32,1,16,128]{3,2,1,0:T(8,128)(2,1)}), bf16[32,1,16,128]{3,2,1,0:T(8,128)(2,1)S(1)}, u32[]{:S(2)}, u32[]{:S(2)}) %all-to-all-start.4) | async-done | bytes 131104 | tf_op jit(solution)/shard_map/cond/branch_0_fun/all_to_all | solution.py:203
  110.7 25.1 %all_to_all.36 = bf16[32,2,16,128]{3,2,1,0:T(8,128)(2,1)S(1)} all-to-all(bf16[32,2,16,128]{3,2,1,0:T(8,128)(2,1)S(1)} %slice.5), channel_id=1, replica_groups=mesh['grp'=16,'seq'=32] {'seq'}, dimensions={0} | all-to-all | bytes 524288 | tf_op jit(solution)/shard_map/cond/branch_0_fun/all_to_all | solution.py:203
  135.9 0.0 copy-done.3
  135.9 0.1 copy.10
  136.0 0.0 copy-done.2
  136.0 0.2 copy.11.router_ref
  136.2 0.0 copy-done
  136.2 0.0 copy-done.1
  136.2 1.5 route.1
  137.8 57.0 %all_to_all.38 = bf16[32,16,1536]{2,1,0:T(8,128)(2,1)S(1)} all-to-all(bf16[32,16,1536]{2,1,0:T(8,128)(2,1)S(1)} %bitcast.14), channel_id=1, replica_groups=mesh['grp'=16,'seq'=32] {'seq'}, dimensions={0} | all-to-all | bytes 3145728 | tf_op jit(solution)/shard_map/all_to_all | solution.py:203
  194.8 0.0 all-gather.5.cloned.1.call-done
  194.8 0.0 all-gather.7.cloned.1.call-done
  194.8 9.8 %mlp.1 = bf16[512,1536]{1,0:T(8,128)(2,1)S(1)} custom-call(bf16[512,1536]{1,0:T(8,128)(2,1)S(1)} %bitcast.13, bf16[2048,1536]{1,0:T(8,128)(2,1)} %bitcast.26, bf16[2048,1536]{1,0:T(8,128)(2,1)} %bitcast.27), custom_call_target="tpu_custom_call" | custom-call | flops 6442450944 | bytes 15728640 | tf_op jit(solution)/shard_map/mlp/pallas_call | solution.py:181
  204.6 57.1 %all_to_all.39 = bf16[32,16,1536]{2,1,0:T(8,128)(2,1)S(1)} all-to-all(bf16[32,16,1536]{2,1,0:T(8,128)(2,1)S(1)} %bitcast.15), channel_id=1, replica_groups=mesh['grp'=16,'seq'=32] {'seq'}, dimensions={0} | all-to-all | bytes 3145728 | tf_op jit(solution)/shard_map/all_to_all | solution.py:203
  261.6 1.8 combine.1
  (2 shorter events, 0.1 us)
Async XLA Ops:
  6.5 188.3 %all-gather.5.cloned.1.call-start = ((), (), s32[]{:S(2)}) async-start(), calls=%async_computation.8 | async-start | bytes 6684672 | tf_op jit(solution)/shard_map/all_gather | solution.py:226
  7.3 187.5 %all-gather.7.cloned.1.call-start = ((), (), s32[]{:S(2)}) async-start(), calls=%async_computation.9 | async-start | bytes 6684672 | tf_op jit(solution)/shard_map/all_gather | solution.py:227
  8.0 43.7 %all-to-all-start.1 = ((bf16[32,3,16,128]{3,2,1,0:T(8,128)(2,1)}), bf16[32,3,16,128]{3,2,1,0:T(8,128)(2,1)S(1)}, u32[]{:S(2)}, u32[]{:S(2)}) async-start(bf16[32,3,16,128]{3,2,1,0:T(8,128)(2,1)} %get-tuple-element.26), calls=%async_computation.1 | async-start | bytes 786432 | tf_op jit(solution)/shard_map/cond/branch_0_fun/all_to_all | solution.py:203
  89.4 46.4 %copy-start.3 = (s32[1,1,128,2]{2,3,1,0:T(2,128)S(1)}, s32[1,1,128,2]{2,3,1,0:T(2,128)}, u32[]{:S(2)}) copy-start(s32[1,1,128,2]{2,3,1,0:T(2,128)} %param.21) | copy-start | bytes 3076
  89.4 46.6 %copy-start.2 = (bf16[1536,32]{0,1:T(8,128)(2,1)S(1)}, bf16[1536,32]{0,1:T(8,128)(2,1)}, u32[]{:S(2)}) copy-start(bf16[1536,32]{0,1:T(8,128)(2,1)} %param.18) | copy-start | bytes 294916
  89.5 46.8 %copy-start = (bf16[8,4,1536]{2,1,0:T(4,128)(2,1)S(1)}, bf16[8,4,1536]{2,1,0:T(4,128)(2,1)}, u32[]{:S(2)}) copy-start(bf16[8,4,1536]{2,1,0:T(4,128)(2,1)} %refs_2_.1) | copy-start | bytes 294916
  89.5 46.8 %copy-start.1 = (bf16[8,16,1536]{2,1,0:T(8,128)(2,1)S(1)}, bf16[8,16,1536]{2,1,0:T(8,128)(2,1)}, u32[]{:S(2)}) copy-start(bf16[8,16,1536]{2,1,0:T(8,128)(2,1)} %res_ref.1) | copy-start | bytes 1179652
  90.2 20.5 %all-to-all-start.4 = ((bf16[32,1,16,128]{3,2,1,0:T(8,128)(2,1)}), bf16[32,1,16,128]{3,2,1,0:T(8,128)(2,1)S(1)}, u32[]{:S(2)}, u32[]{:S(2)}) async-start(bf16[32,1,16,128]{3,2,1,0:T(8,128)(2,1)} %slice.4), calls=%async_computation.4 | async-start | bytes 262144 | tf_op jit(solution)/shard_map/cond/branch_0_fun/all_to_all | solution.py:203
Sparse Core Ops, SparseCore 0:
  9.5 64.5 all-gather.4
  76.3 56.7 all-gather.6

commit v5 on v4

--- a/solution.py
+++ b/solution.py
@@ -12,8 +12,9 @@
 bf16 = jnp.bfloat16
 
 
-def attention_kernel(qkv_ref, o_ref):
-    blocks, pairs, rows, width = o_ref.shape
+def attention_kernel(qkv_ref, first_ref, rest_ref):
+    blocks, others, rows, width = rest_ref.shape
+    pairs = others + 1
     length = blocks * rows
     scale = 1.0 / math.sqrt(width)
     for i in range(pairs):
@@ -23,7 +24,8 @@
         powers = jnp.exp((scores - top) * scale)
         total = jnp.sum(powers, axis=1, keepdims=True)
         out = jnp.dot(powers.astype(bf16), v, preferred_element_type=f32) * (1.0 / total)
-        o_ref[:, i] = out.astype(bf16).reshape(blocks, rows, width)
+        ref, place = (first_ref, 0) if i == 0 else (rest_ref, i - 1)
+        ref[:, place] = out.astype(bf16).reshape(blocks, rows, width)
 
 
 def attend(qkv):
@@ -32,7 +34,9 @@
     length = blocks * rows
     return pl.pallas_call(
         attention_kernel,
-        out_shape=jax.ShapeDtypeStruct((blocks, pairs, rows, width), bf16),
+        out_shape=tuple(
+            jax.ShapeDtypeStruct((blocks, part, rows, width), bf16) for part in (1, pairs - 1)
+        ),
         compiler_params=pltpu.CompilerParams(vmem_limit_bytes=32 * 2**20),
         cost_estimate=pl.CostEstimate(
             flops=4 * pairs * length * length * width,
@@ -240,10 +244,13 @@
     qkv = lax.cond(
         core == 0, together, apart, arrange(query_heads), arrange(key_heads), arrange(value_heads)
     )
-    def by_pair(pairs):
-        return jnp.concatenate([swap(pairs[:, :1]), swap(pairs[:, 1:])], axis=1)
-
-    attn = lax.cond(core == 0, swap, by_pair, attend(qkv)).reshape(
+    def at_once(first, rest):
+        return swap(jnp.concatenate([first, rest], axis=1))
+
+    def by_pair(first, rest):
+        return jnp.concatenate([swap(first), swap(rest)], axis=1)
+
+    attn = lax.cond(core == 0, at_once, by_pair, *attend(qkv)).reshape(
         seqs_dev, head_count, len_dev, head_width
     )
     stream, outbound, gates = route(attn, residual, modulation, router, ids)

time: 271 us -> 274 us (1.011)
  blocking collectives: 175 us -> 200 us
  waiting for transfers between devices: 41.2 us -> 25.4 us
  starting transfers between devices: 23.2 us -> 18.5 us
    all_to_all x4 -> x5, blocking collectives: 175 us -> 200 us  [swap(): lax.all_to_all(blocks, 'seq', split_axis=0, concat_axis=0, tiled=True)]
    all_to_all x2 -> x1, waiting for transfers between devices: 39.8 us -> 23.9 us  [swap(): lax.all_to_all(blocks, 'seq', split_axis=0, concat_axis=0, tiled=True)]
    all_to_all x2 -> x1, starting transfers between devices: 23.1 us -> 18.5 us  [swap(): lax.all_to_all(blocks, 'seq', split_axis=0, concat_axis=0, tiled=True)]
  transfers between devices with their start and end apart: 4 -> 3, of which waited for: 2 -> 1; matrix products, arithmetic and copies ran while one was open for 1% -> 1% of each run, Pallas kernels for 1% -> 1%
where the time goes in v5:
time: 274 us; the launch traced here: 273 us
  blocking collectives  200 us (73%)
  waiting for transfers between devices  25.4 us (9%)
  starting transfers between devices  18.5 us (7%)
  Pallas kernels  14.4 us (5%)
  between operations  13.5 us (5%)
    all_to_all x5, blocking collectives, swap(): lax.all_to_all(blocks, 'seq', split_axis=0, concat_axis=0, tiled=True)  200 us
    all_to_all x1, waiting for transfers between devices, swap(): lax.all_to_all(blocks, 'seq', split_axis=0, concat_axis=0, tiled=True)  23.9 us
    all_to_all x1, starting transfers between devices, swap(): lax.all_to_all(blocks, 'seq', split_axis=0, concat_axis=0, tiled=True)  18.5 us
    pallas_call x1, Pallas kernels, mlp(): pl.pallas_call(mlp_kernel, grid=(tiles + 1,), in_specs=[pl.BlockSpec((cou...  9.76 us
  transfers between devices with their start and end apart: 3, of which 1 were waited for; matrix products, arithmetic and copies ran while one was open for 1% of the time, Pallas kernels for 1%

profile of v5, /device:TPU:1, one launch (start us, length us, event | category | flops | bytes accessed | tf_op | source)
XLA Modules:
  0.0 273.2 jit_solution(13127171886223237057)
XLA Ops:
  6.5 0.0 all-gather.5.cloned.1.call-start
  6.5 0.7 all-gather.5.cloned.1.call-update
  7.3 0.0 all-gather.7.cloned.1.call-start
  7.3 0.7 all-gather.7.cloned.1.call-update
  8.0 80.0 %conditional.2 = (bf16[32,9,16,128]{3,2,1,0:T(8,128)(2,1)S(1)}) conditional(s32[]{:T(128)} %convert_element_type.4, (bf16[32,3,16,128]{3,2,1,0:T(8,128)(2,1)}, bf16[32,3,16,128]{3,2,1,0:T(8,128)(2,1)}, bf16[32,3,16,128]{3,2,1,0:T(8,128)(2,1)}) %tuple.30, (bf16[32,3,16,128]{3,2,1,0:T(8,128)(2,1)}, bf16[32,3,16,128]{3,2,1,0:T(8,128)(2,1)}, ...), branch_computations={%region_0.1_spmd, %region_1.2_spmd} | conditional | flops 1179648 | bytes 6684712 | solution.py:244
  8.0 18.5 %all-to-all-start = ((bf16[32,3,16,128]{3,2,1,0:T(8,128)(2,1)}), bf16[32,3,16,128]{3,2,1,0:T(8,128)(2,1)S(1)}, u32[]{:S(2)}, u32[]{:S(2)}) async-start(bf16[32,3,16,128]{3,2,1,0:T(8,128)(2,1)} %get-tuple-element.32), calls=%async_computation | async-start | bytes 786432 | tf_op jit(solution)/shard_map/cond/branch_0_fun/all_to_all | solution.py:207
  26.5 1.2 pad_maximum_fusion.1
  27.7 23.9 %all-to-all-done = bf16[32,3,16,128]{3,2,1,0:T(8,128)(2,1)S(1)} async-done(((bf16[32,3,16,128]{3,2,1,0:T(8,128)(2,1)}), bf16[32,3,16,128]{3,2,1,0:T(8,128)(2,1)S(1)}, u32[]{:S(2)}, u32[]{:S(2)}) %all-to-all-start) | async-done | bytes 393248 | tf_op jit(solution)/shard_map/cond/branch_0_fun/all_to_all | solution.py:207
  51.7 36.2 %all_to_all.34 = bf16[32,6,16,128]{3,2,1,0:T(8,128)(2,1)S(1)} all-to-all(bf16[32,6,16,128]{3,2,1,0:T(8,128)(2,1)S(1)} %pad_maximum_fusion.1), channel_id=1, replica_groups=mesh['grp'=16,'seq'=32] {'seq'}, dimensions={0} | all-to-all | bytes 1572864 | tf_op jit(solution)/shard_map/cond/branch_0_fun/all_to_all | solution.py:207
  87.9 0.1 pad_maximum_fusion
  88.0 1.4 attend.1
  89.4 0.0 copy-start.3
  89.4 0.0 copy-start.2
  89.5 0.0 copy-start
  89.5 0.0 copy-start.1
  89.5 46.5 %conditional.3 = (bf16[8,12,16,128]{3,2,1,0:T(8,128)(2,1)S(1)}) conditional(s32[]{:T(128)} %convert_element_type.4, (bf16[32,1,16,128]{3,2,1,0:T(8,128)(2,1)S(1)}, bf16[32,2,16,128]{3,2,1,0:T(8,128)(2,1)S(1)}) %attend.1, (bf16[32,1,16,128]{3,2,1,0:T(8,128)(2,1)S(1)}, bf16[32,2,16,128]{3,2,1,0:T(8,128)(2,1)S(1)}) %attend.1), branch_computations={%region_2.3_spmd, %region_3.4_spmd} | conditional | flops 196608 | bytes 1572872 | solution.py:253
  89.5 20.5 %all_to_all.36 = bf16[32,1,16,128]{3,2,1,0:T(8,128)(2,1)S(1)} all-to-all(bf16[32,1,16,128]{3,2,1,0:T(8,128)(2,1)S(1)} %get-tuple-element.38), channel_id=1, replica_groups=mesh['grp'=16,'seq'=32] {'seq'}, dimensions={0} | all-to-all | bytes 262144 | tf_op jit(solution)/shard_map/cond/branch_0_fun/all_to_all | solution.py:207
  110.0 26.0 %all_to_all.37 = bf16[32,2,16,128]{3,2,1,0:T(8,128)(2,1)S(1)} all-to-all(bf16[32,2,16,128]{3,2,1,0:T(8,128)(2,1)S(1)} %get-tuple-element.39), channel_id=1, replica_groups=mesh['grp'=16,'seq'=32] {'seq'}, dimensions={0} | all-to-all | bytes 524288 | tf_op jit(solution)/shard_map/cond/branch_0_fun/all_to_all | solution.py:207
  136.0 0.0 copy-done.3
  136.0 0.1 copy.10
  136.1 0.0 copy-done.2
  136.2 0.2 copy.11.router_ref
  136.4 0.0 copy-done
  136.4 0.0 copy-done.1
  136.4 1.5 route.1
  137.9 57.3 %all_to_all.39 = bf16[32,16,1536]{2,1,0:T(8,128)(2,1)S(1)} all-to-all(bf16[32,16,1536]{2,1,0:T(8,128)(2,1)S(1)} %bitcast.14), channel_id=1, replica_groups=mesh['grp'=16,'seq'=32] {'seq'}, dimensions={0} | all-to-all | bytes 3145728 | tf_op jit(solution)/shard_map/all_to_all | solution.py:207
  195.3 0.0 all-gather.5.cloned.1.call-done
  195.3 0.0 all-gather.7.cloned.1.call-done
  195.3 9.8 %mlp.1 = bf16[512,1536]{1,0:T(8,128)(2,1)S(1)} custom-call(bf16[512,1536]{1,0:T(8,128)(2,1)S(1)} %bitcast.13, bf16[2048,1536]{1,0:T(8,128)(2,1)} %bitcast.26, bf16[2048,1536]{1,0:T(8,128)(2,1)} %bitcast.27), custom_call_target="tpu_custom_call" | custom-call | flops 6442450944 | bytes 15728640 | tf_op jit(solution)/shard_map/mlp/pallas_call | solution.py:185
  205.0 59.5 %all_to_all.40 = bf16[32,16,1536]{2,1,0:T(8,128)(2,1)S(1)} all-to-all(bf16[32,16,1536]{2,1,0:T(8,128)(2,1)S(1)} %bitcast.15), channel_id=1, replica_groups=mesh['grp'=16,'seq'=32] {'seq'}, dimensions={0} | all-to-all | bytes 3145728 | tf_op jit(solution)/shard_map/all_to_all | solution.py:207
  264.6 1.8 combine.1
  (1 shorter events, 0.0 us)
Async XLA Ops:
  6.5 188.7 %all-gather.5.cloned.1.call-start = ((), (), s32[]{:S(2)}) async-start(), calls=%async_computation.8 | async-start | bytes 6684672 | tf_op jit(solution)/shard_map/all_gather | solution.py:230
  7.3 188.0 %all-gather.7.cloned.1.call-start = ((), (), s32[]{:S(2)}) async-start(), calls=%async_computation.9 | async-start | bytes 6684672 | tf_op jit(solution)/shard_map/all_gather | solution.py:231
  8.0 43.7 %all-to-all-start = ((bf16[32,3,16,128]{3,2,1,0:T(8,128)(2,1)}), bf16[32,3,16,128]{3,2,1,0:T(8,128)(2,1)S(1)}, u32[]{:S(2)}, u32[]{:S(2)}) async-start(bf16[32,3,16,128]{3,2,1,0:T(8,128)(2,1)} %get-tuple-element.32), calls=%async_computation | async-start | bytes 786432 | tf_op jit(solution)/shard_map/cond/branch_0_fun/all_to_all | solution.py:207
  89.4 46.6 %copy-start.3 = (s32[1,1,128,2]{2,3,1,0:T(2,128)S(1)}, s32[1,1,128,2]{2,3,1,0:T(2,128)}, u32[]{:S(2)}) copy-start(s32[1,1,128,2]{2,3,1,0:T(2,128)} %param.21) | copy-start | bytes 3076
  89.4 46.7 %copy-start.2 = (bf16[1536,32]{0,1:T(8,128)(2,1)S(1)}, bf16[1536,32]{0,1:T(8,128)(2,1)}, u32[]{:S(2)}) copy-start(bf16[1536,32]{0,1:T(8,128)(2,1)} %param.18) | copy-start | bytes 294916
  89.5 46.9 %copy-start = (bf16[8,4,1536]{2,1,0:T(4,128)(2,1)S(1)}, bf16[8,4,1536]{2,1,0:T(4,128)(2,1)}, u32[]{:S(2)}) copy-start(bf16[8,4,1536]{2,1,0:T(4,128)(2,1)} %refs_2_.1) | copy-start | bytes 294916
  89.5 46.9 %copy-start.1 = (bf16[8,16,1536]{2,1,0:T(8,128)(2,1)S(1)}, bf16[8,16,1536]{2,1,0:T(8,128)(2,1)}, u32[]{:S(2)}) copy-start(bf16[8,16,1536]{2,1,0:T(8,128)(2,1)} %res_ref.1) | copy-start | bytes 1179652
Sparse Core Ops, SparseCore 0:
  9.5 64.5 all-gather.4
  76.3 56.4 all-gather.6
